TPU v7x, 512 devices: a whole 4x8x8 slice. The times are simulated.
512 devices in a mesh: rep: 16 (over x, y_hi), fsdp: 32 (over z, y_lo, core).
Axes of the slice: x: 4, y: 8 (y_hi: 4, y_lo: 2; y = y_hi * 2 + y_lo), z: 8, core: 2. Of those that a mesh axis runs over, the one named last changes fastest.
Arguments:
- partial_grads: bfloat16 [16, 32, 1, 64, 12288], P('rep', 'fsdp'), may hold values from -3 to 3
- momentum: float32 [16, 1, 64, 12288], P('rep', None, None, 'fsdp'), may hold values from -6 to 6
- keep_index: int32 [1, 1, 192, 32], P(None, None, 'fsdp'), may hold values from 0 to 4095, as said below
Outputs:
- new_momentum: float32 [16, 1, 64, 12288], P('rep', None, None, 'fsdp')
- update: float32 [1, 64, 12288], P(None, None, 'fsdp')
Inputs may be any that keep to these rules, and one draw needn't show every extreme that they name: `keep_index`: the 32 numbers of each block are distinct.
All inputs are finite; a program needn't handle non-finite values.
Results may differ from a plain program's by a relative error of at most 0.0003.
Values sent between devices are 32-bit elements; how exact they have to be, the bound alone decides.
No kernel may reach another device: no remote copies, remote signals or barrier semaphores. Data moves between devices by JAX's collectives and lax.ppermute only.
A program may use at most 64 MiB of HBM per device.

v0:
```python
import jax
import jax.numpy as jnp
from jax import lax
from jax.sharding import PartitionSpec as P

BLOCK = 64


BETA_DECAY = 0.999
SOFTNESS = 0.02


def dct_matrix(block_size):
    frequency = jnp.arange(block_size, dtype=jnp.float32)[:, None]
    sample = jnp.arange(block_size, dtype=jnp.float32)[None, :]
    weights = jnp.where(frequency == 0, jnp.sqrt(1.0 / block_size), jnp.sqrt(2.0 / block_size))
    return weights * jnp.cos(jnp.pi * (2.0 * sample + 1.0) * frequency / (2.0 * block_size))


def to_blocks(field_in, block_size):
    lead_dims = field_in.shape[:-2]
    row_blocks = field_in.shape[-2] // block_size
    col_blocks = field_in.shape[-1] // block_size
    reshaped = field_in.reshape(lead_dims + (row_blocks, block_size, col_blocks, block_size))
    return jnp.swapaxes(reshaped, -3, -2)


def from_blocks(blocked):
    lead_dims = blocked.shape[:-4]
    row_blocks = blocked.shape[-4]
    col_blocks = blocked.shape[-3]
    block_size = blocked.shape[-1]
    return jnp.swapaxes(blocked, -3, -2).reshape(
        lead_dims + (row_blocks * block_size, col_blocks * block_size)
    )


def forward_dct(blocked, dct_table):
    return jnp.einsum(
        "kn,...nm,jm->...kj", dct_table, blocked, dct_table, precision=lax.Precision.HIGHEST
    )


def inverse_dct(coeffs, dct_table):
    return jnp.einsum(
        "kn,...kj,jm->...nm", dct_table, coeffs, dct_table, precision=lax.Precision.HIGHEST
    )


def extract(gradient, momentum, keep_index, dct_table):
    block_size = dct_table.shape[0]
    updated = BETA_DECAY * momentum + gradient
    coeffs = forward_dct(to_blocks(updated, block_size), dct_table)
    flat_coeffs = coeffs.reshape(coeffs.shape[:-2] + (block_size * block_size,))
    one_hot = (
        keep_index[..., None] == jnp.arange(block_size * block_size, dtype=jnp.int32)
    ).astype(jnp.float32)
    kept_mask = jnp.sum(one_hot, axis=-2)
    wanted = jnp.broadcast_to(keep_index, flat_coeffs.shape[:-1] + (keep_index.shape[-1],))
    kept_values = jnp.take_along_axis(flat_coeffs, wanted, axis=-1)
    rebuilt = inverse_dct((flat_coeffs * kept_mask).reshape(coeffs.shape), dct_table)
    return (updated - from_blocks(rebuilt), kept_values, one_hot)


def finish(averaged, one_hot, dct_table):
    block_size = dct_table.shape[0]
    coeff_grid = jnp.einsum("...k,...kj->...j", averaged, one_hot, precision=lax.Precision.HIGHEST)
    blocked = inverse_dct(
        coeff_grid.reshape(coeff_grid.shape[:-1] + (block_size, block_size)), dct_table
    )
    direction = from_blocks(blocked)
    return direction / jnp.sqrt(direction * direction + SOFTNESS * SOFTNESS)


def per_device(partial_grads, momentum, keep_index):
    dct_table = dct_matrix(BLOCK)
    gradient = lax.psum_scatter(
        partial_grads.astype(jnp.float32), "fsdp", scatter_dimension=4, tiled=True
    )[0]
    new_momentum, kept_values, one_hot = extract(gradient, momentum, keep_index, dct_table)
    collected = lax.all_gather(kept_values, "rep", axis=0, tiled=True)
    averaged = jnp.sum(collected, axis=0) / lax.axis_size("rep")
    return (new_momentum, finish(averaged, one_hot, dct_table))


def solution(mesh):
    in_specs = (
        P("rep", "fsdp", None, None, None),
        P("rep", None, None, "fsdp"),
        P(None, None, "fsdp", None),
    )
    out_specs = (P("rep", None, None, "fsdp"), P(None, None, "fsdp"))
    return jax.shard_map(
        per_device, mesh=mesh, in_specs=in_specs, out_specs=out_specs, check_vma=False
    )
```

profile of v0, /device:TPU:16, one launch (start us, length us, event | category | flops | bytes accessed | tf_op | source)
XLA Modules:
  0.0 194.3 jit_solution(13655750318760409826)
XLA Ops:
  7.2 0.0 copy-start.1
  7.2 0.0 copy-start
  7.2 0.0 reduce-scatter.2.cloned.1.call-start
  7.2 3.3 %convert_element_type.14 = f32[1,1,1,64,12288]{4,3,2,1,0:T(8,128)} convert(bf16[1,1,1,64,12288]{4,3,2,1,0:T(8,128)(2,1)} %param.3) | non-fusion elementwise | flops 786432 | bytes 4718592 | tf_op jit(solution)/shard_map/convert_element_type | solution.py:78
  10.5 0.0 reduce-scatter.2.cloned.1.call-update
  10.5 0.0 copy-done.1
  10.6 0.6 convert_reduce_fusion
  11.2 0.1 broadcast_in_dim.28
  11.3 0.1 reshape.250
  11.4 127.5 %reduce-scatter.2.cloned.1.call-done = f32[1,1,1,64,384]{4,3,2,1,0:T(8,128)} async-done(((f32[1,1,1,64,12288]{4,3,2,1,0:T(8,128)}), f32[1,1,1,64,384]{4,3,2,1,0:T(8,128)}) %reduce-scatter.2.cloned.1.call-update) | async-done | bytes 98320 | tf_op jit(solution)/shard_map/reduce_scatter | solution.py:77
  138.9 0.0 copy-done
  138.9 0.9 bitcast_add_fusion
  139.8 0.1 reshape.238
  139.9 0.5 fusion.2
  140.4 0.4 fusion.11
  140.9 0.1 reshape.248
  141.0 0.5 fusion.4
  141.5 0.4 convolution_bitcast_fusion.1
  141.9 0.1 copy.26
  142.0 0.1 reshape.240
  142.1 0.7 sub.3
  142.8 1.6 gather_fusion
  144.4 0.1 reshape.245
  144.5 39.8 %all_gather.3 = f32[16,1,1,6,32]{4,2,3,1,0:T(1,128)S(1)} all-gather(f32[1,1,1,6,32]{4,2,3,1,0:T(1,128)S(1)} %and_select_fusion), channel_id=1, replica_groups=mesh['rep'=16,'fsdp'=32] {'rep'}, dimensions={0}, use_global_device_ids=true | all-gather | bytes 13056 | tf_op jit(solution)/shard_map/all_gather | solution.py:81
  184.2 0.1 reduce_sum.19
  184.3 1.1 fusion
  185.5 0.1 copy.44
  185.5 0.1 reshape.242
  185.6 0.5 fusion.7
  186.1 0.4 convolution_bitcast_fusion
  186.6 0.1 copy.29
  186.7 0.1 reshape.243
  186.8 0.7 rsqrt_multiply_fusion
  (5 shorter events, 0.1 us)
Async XLA Ops:
  7.2 3.4 %copy-start.1 = (s32[1,1,6,32]{3,1,2,0:T(1,128)S(1)}, s32[1,1,6,32]{3,1,2,0:T(1,128)}, u32[]{:S(2)}) copy-start(s32[1,1,6,32]{3,1,2,0:T(1,128)} %param.5) | copy-start | bytes 2308
  7.2 131.8 %copy-start = (f32[1,1,64,384]{3,2,1,0:T(8,128)S(1)}, f32[1,1,64,384]{3,2,1,0:T(8,128)}, u32[]{:S(2)}) copy-start(f32[1,1,64,384]{3,2,1,0:T(8,128)} %param.4) | copy-start | bytes 294916
  7.2 131.7 %reduce-scatter.2.cloned.1.call-start = ((), (), s32[]{:S(2)}) async-start(), calls=%async_computation.1 | async-start | bytes 3244032 | tf_op jit(solution)/shard_map/reduce_scatter | solution.py:77
Sparse Core Ops, SparseCore 0:
  10.8 128.0 reduce-scatter.1
where the time goes:
time: 194 us
  waiting for transfers between devices  128 us (66%)
  blocking collectives  39.8 us (21%)
  between operations  14.2 us (7%)
  other arithmetic  6.23 us (3%)
  matrix products  3.91 us (2%)
  local copies, waits for them, and re-layouts  2.64 us (1%)
    reduce_scatter x1, waiting for transfers between devices, per_device(): lax.psum_scatter(partial_grads.astype(jnp.float32), 'fsdp', scatter_dimen...  128 us
    all_gather x1, blocking collectives, per_device(): collected = lax.all_gather(kept_values, 'rep', axis=0, tiled=True)  39.8 us
  transfers between devices with their start and end apart: 1, of which 1 were waited for; matrix products, arithmetic and copies ran while one was open for 0% of the time, Pallas kernels for 0%

commit v1 on v0

v1 whole, which is shorter than its diff:
```python
import functools

import jax
import jax.numpy as jnp
import numpy as np
from jax import lax
from jax.experimental import pallas as pl
from jax.experimental.pallas import tpu as pltpu
from jax.sharding import Mesh
from jax.sharding import PartitionSpec as P

BLOCK = 64
BETA_DECAY = 0.999
SOFTNESS = 0.02
WIDE = 384
PAIRS = WIDE // 128
KEPT = 64
SIZES = {"x": 4, "yh": 4, "z": 8, "yl": 2, "c": 2}
REP = ("x", "yh")
FSDP = ("z", "yl", "c")
SLOTS = ((0, 4), (0, 3), (1, 3), (0, 2), (1, 2), (0, 1), (1, 1), (0, 0))
HIGHEST = lax.Precision.HIGHEST


def dct_matrix():
    k = np.arange(BLOCK)[:, None]
    n = np.arange(BLOCK)[None, :]
    scale = np.where(k == 0, np.sqrt(1.0 / BLOCK), np.sqrt(2.0 / BLOCK))
    return (scale * np.cos(np.pi * (2 * n + 1) * k / (2 * BLOCK))).astype(np.float32)


def dot(a, b):
    return jnp.dot(a, b, precision=HIGHEST, preferred_element_type=jnp.float32)


def dot_nt(a, b):
    return lax.dot_general(
        a, b, (((1,), (1,)), ((), ())), precision=HIGHEST, preferred_element_type=jnp.float32
    )


def vmem():
    return pl.BlockSpec(memory_space=pltpu.VMEM)


def f32(*shape):
    return jax.ShapeDtypeStruct(shape, jnp.float32)


def params():
    return pltpu.CompilerParams(vmem_limit_bytes=32 * 1024 * 1024)


def chunks(grads_ref, core):
    z = lax.axis_index("z")
    yl = lax.axis_index("yl")
    for slot, (part, distance) in enumerate(SLOTS):
        target = lax.rem(z + 8 + (1 - 2 * core) * distance, 8)
        part = core if part == 0 else 1 - core
        for side in range(2):
            block = 4 * target + 2 * (yl if side == 0 else 1 - yl) + part
            start = pl.multiple_of(block * WIDE, 128)
            yield slot, side, grads_ref[:, pl.ds(start, WIDE)].astype(jnp.float32)


def split_kernel(grads_ref, give_ref, own_ref):
    core = lax.axis_index("c")
    for slot, side, columns in chunks(grads_ref, 1 - core):
        give_ref[slot, side] = columns
    for slot, side, columns in chunks(grads_ref, core):
        own_ref[slot, side] = columns


def split(grads):
    return pl.pallas_call(
        split_kernel,
        out_shape=(f32(len(SLOTS), 2, BLOCK, WIDE),) * 2,
        in_specs=[vmem()],
        out_specs=(vmem(),) * 2,
        compiler_params=params(),
    )(grads)


def table_kernel(index_ref, dct_ref, rows_ref, cols_ref, rows_t_ref):
    dct = dct_ref[...]
    index = index_ref[...]
    size = index.shape[-1]
    iota = lax.broadcasted_iota(jnp.int32, (BLOCK, size), 0)
    hot_u = (iota == lax.shift_right_logical(index, 6)).astype(jnp.float32)
    hot_v = (iota == jnp.bitwise_and(index, 63)).astype(jnp.float32)
    rows_t_ref[...] = dot(dct.T, hot_u)
    rows_ref[...] = dot(hot_u.T, dct)
    wide = dot(hot_v.T, jnp.concatenate([dct, dct], axis=1))
    row = lax.broadcasted_iota(jnp.int32, (size, 128), 0)
    lane = lax.broadcasted_iota(jnp.int32, (size, 128), 1)
    mine = jnp.bitwise_and(lax.shift_right_logical(row, 5), 1) == lax.shift_right_logical(lane, 6)
    cols_ref[...] = jnp.where(mine, wide, 0.0)


def tables(index):
    size = index.shape[-1]
    return pl.pallas_call(
        table_kernel,
        out_shape=(f32(size, BLOCK), f32(size, 128), f32(BLOCK, size)),
        in_specs=[vmem()] * 2,
        out_specs=(vmem(),) * 3,
        compiler_params=params(),
    )(index, dct_matrix())


def join_kernel(own_ref, got_ref, three_ref, four_ref, two_ref, near_ref, near_x_ref, here_ref):
    for ref, first in ((three_ref, 1), (two_ref, 3)):
        for part in range(2):
            ref[part] = own_ref[first + part] + got_ref[first + part]
    for ref, slot in ((four_ref, 0), (near_ref, 5), (near_x_ref, 6), (here_ref, 7)):
        ref[...] = own_ref[slot] + got_ref[slot]


def join(own, got):
    pair = f32(2, BLOCK, WIDE)
    quad = f32(2, 2, BLOCK, WIDE)
    return pl.pallas_call(
        join_kernel,
        out_shape=(quad, pair, quad, pair, pair, pair),
        in_specs=[vmem()] * 2,
        out_specs=(vmem(),) * 6,
        compiler_params=params(),
    )(own, got)


def add_kernel(parts, *refs):
    *ins, out = refs
    terms = [r[...] if p is None else r[p] for r, p in zip(ins, parts)]
    out[...] = functools.reduce(jnp.add, terms)


def add(*terms):
    return pl.pallas_call(
        functools.partial(add_kernel, [p for _, p in terms]),
        out_shape=f32(2, BLOCK, WIDE),
        in_specs=[vmem()] * len(terms),
        out_specs=vmem(),
        compiler_params=params(),
    )(*[a for a, _ in terms])


def merge_kernel(*refs):
    *ins, mine, other = refs
    for side, out in enumerate((mine, other)):
        out[...] = functools.reduce(jnp.add, [r[side] for r in ins])


def merge(*terms):
    return pl.pallas_call(
        merge_kernel,
        out_shape=(f32(BLOCK, WIDE),) * 2,
        in_specs=[vmem()] * len(terms),
        out_specs=(vmem(),) * 2,
        compiler_params=params(),
    )(*terms)


def forward(field, rows, cols):
    total = jnp.zeros((8, KEPT), jnp.float32)
    row = lax.broadcasted_iota(jnp.int32, (8, 128), 0)
    for p in range(PAIRS):
        span = slice(p * KEPT, (p + 1) * KEPT)
        product = dot(rows[span], field[:, p * 128 : (p + 1) * 128]) * cols[span]
        total = total + dot_nt((row == p).astype(jnp.float32), product)
    return total


def inverse(kept, rows_t, cols, p):
    span = slice(p * KEPT, (p + 1) * KEPT)
    return dot(rows_t[:, span] * kept[p : p + 1, :KEPT], cols[span])


def extract_kernel(*refs):
    *terms, momentum_ref, rows_ref, cols_ref, rows_t_ref, new_ref, kept_ref = refs
    updated = functools.reduce(jnp.add, [r[...] for r in terms]) + BETA_DECAY * momentum_ref[...]
    kept = forward(updated, rows_ref, cols_ref)
    tile = jnp.concatenate([kept, jnp.zeros((8, 128 - KEPT), jnp.float32)], axis=1)
    for r in range(kept_ref.shape[0]):
        kept_ref[r] = tile
    for p in range(PAIRS):
        span = slice(p * 128, (p + 1) * 128)
        new_ref[:, span] = updated[:, span] - inverse(kept, rows_t_ref, cols_ref, p)


def extract(groups, *args):
    return pl.pallas_call(
        extract_kernel,
        out_shape=(f32(BLOCK, WIDE), f32(groups, 8, 128)),
        in_specs=[vmem()] * len(args),
        out_specs=(vmem(),) * 2,
        compiler_params=params(),
    )(*args)


def finish_kernel(all_ref, cols_ref, rows_t_ref, upd_ref):
    averaged = jnp.sum(all_ref[...], axis=0) * (1.0 / all_ref.shape[0])
    for p in range(PAIRS):
        direction = inverse(averaged, rows_t_ref, cols_ref, p)
        upd_ref[:, p * 128 : (p + 1) * 128] = direction * lax.rsqrt(
            direction * direction + SOFTNESS * SOFTNESS
        )


def finish(*args):
    return pl.pallas_call(
        finish_kernel,
        out_shape=f32(BLOCK, WIDE),
        in_specs=[vmem()] * 3,
        out_specs=vmem(),
        compiler_params=params(),
    )(*args)


def permutation(hops, flip_yl, flip_c):
    flat = lambda z, yl, c: (z % 8) * 4 + yl * 2 + c
    return [
        (flat(z, yl, c), flat(z + hops * (1 - 2 * c), yl ^ flip_yl, c ^ flip_c))
        for z in range(8)
        for yl in range(2)
        for c in range(2)
    ]


def send(array, hops=0, yl=0, c=0):
    return lax.ppermute(array, FSDP, permutation(hops, yl, c))


def per_device(partial_grads, momentum, keep_index):
    grads = partial_grads.reshape(BLOCK, -1)
    momentum = momentum.reshape(BLOCK, WIDE)

    give, own = split(grads)
    got = send(give, c=1)
    rows, cols, rows_t = tables(keep_index.reshape(1, -1))
    three, four, two, near, near_x, here = join(own, got)
    three = send(three, hops=1)
    four = send(four, hops=2)
    near = send(near, hops=1)
    near_x = send(near_x, hops=1, c=1)
    far_x = send(add((two, 1), (three, 1)), hops=2, c=1)
    far = send(add((two, 0), (three, 0), (four, None)), hops=2)
    mine, other = merge(here, near, near_x, far, far_x)
    other = send(other, yl=1)

    groups = SIZES["x"] * SIZES["yh"]
    new_momentum, kept = extract(groups, mine, other, momentum, rows, cols, rows_t)
    kept = lax.all_to_all(kept, REP, 0, 0, tiled=True)
    update = finish(kept, cols, rows_t)
    return new_momentum.reshape(1, 1, BLOCK, WIDE), update.reshape(1, BLOCK, WIDE)


def solution(mesh):
    inner = Mesh(mesh.devices.reshape(tuple(SIZES.values())), tuple(SIZES))
    in_specs = (
        P(REP, FSDP, None, None, None),
        P(REP, None, None, FSDP),
        P(None, None, FSDP, None),
    )
    out_specs = (P(REP, None, None, FSDP), P(None, None, FSDP))
    return jax.shard_map(
        per_device, mesh=inner, in_specs=in_specs, out_specs=out_specs, check_vma=False
    )
```

time: 194 us -> 72.5 us (0.37)
  the two profiles are of different devices: /device:TPU:16 before, /device:TPU:1 now
where the time goes in v1:
time: 72.5 us; the launch traced here: 72.1 us
  starting transfers between devices  33.3 us (46%)
  blocking collectives  18.7 us (26%)
  waiting for transfers between devices  14.3 us (20%)
  Pallas kernels  3.49 us (5%)
  local copies, waits for them, and re-layouts  1.49 us (2%)
  between operations  0.77 us (1%)
    ppermute x8, starting transfers between devices, send(): return lax.ppermute(array, FSDP, permutation(hops, yl, c))  33.3 us
    all_to_all x1, blocking collectives, per_device(): kept = lax.all_to_all(kept, REP, 0, 0, tiled=True)  18.7 us
    ppermute x8, waiting for transfers between devices, send(): return lax.ppermute(array, FSDP, permutation(hops, yl, c))  14.3 us
    pallas_call x1, Pallas kernels, extract(): pl.pallas_call(extract_kernel, out_shape=(f32(BLOCK, WIDE), f32(groups, 8...  1.61 us
  transfers between devices with their start and end apart: 8, of which 5 were waited for; matrix products, arithmetic and copies ran while one was open for 0% of the time, Pallas kernels for 1%

profile of v1, /device:TPU:1, one launch (start us, length us, event | category | flops | bytes accessed | tf_op | source)
XLA Modules:
  0.0 72.1 jit_solution(10164890857187781522)
XLA Ops:
  0.6 0.0 copy-start
  0.6 1.4 %copy-done = bf16[1,1,1,64,12288]{4,3,2,1,0:T(8,128)(2,1)S(1)} copy-done((bf16[1,1,1,64,12288]{4,3,2,1,0:T(8,128)(2,1)S(1)}, bf16[1,1,1,64,12288]{4,3,2,1,0:T(8,128)(2,1)}, u32[]{:S(2)}) %copy-start) | copy-done | bytes 1572888
  2.0 0.2 shard_map.59
  2.2 8.8 %collective-permute-start = (f32[8,2,64,384]{3,2,1,0:T(8,128)S(1)}, f32[8,2,64,384]{3,2,1,0:T(8,128)S(1)}, u32[]{:S(2)}, u32[]{:S(2)}) collective-permute-start(f32[8,2,64,384]{3,2,1,0:T(8,128)S(1)} %get-tuple-element.18), channel_id=1, source_target_pairs={{0,1},{1,0},{2,3},{3,2},{4,5},{5,4},{6,7},{7,6},{8,9},{9,8},{10,11... | collective-permute-start | bytes 4718600 | tf_op jit(solution)/shard_map/ppermute | solution.py:230
  11.0 3.0 %collective-permute-done.got_ref = f32[8,2,64,384]{3,2,1,0:T(8,128)S(1)} collective-permute-done((f32[8,2,64,384]{3,2,1,0:T(8,128)S(1)}, f32[8,2,64,384]{3,2,1,0:T(8,128)S(1)}, u32[]{:S(2)}, u32[]{:S(2)}) %collective-permute-start) | collective-permute-done | bytes 1572896 | tf_op jit(solution)/shard_map/ppermute | solution.py:230
  14.1 0.2 shard_map.60
  14.2 5.3 %collective-permute-start.3 = (f32[2,2,64,384]{3,2,1,0:T(8,128)S(1)}, f32[2,2,64,384]{3,2,1,0:T(8,128)S(1)}, u32[]{:S(2)}, u32[]{:S(2)}) collective-permute-start(f32[2,2,64,384]{3,2,1,0:T(8,128)S(1)} %get-tuple-element.23), channel_id=1, source_target_pairs={{0,4},{1,29},{2,6},{3,31},{4,8},{5,1},{6,10},{7,3},{8,12},{9,5},{1... | collective-permute-start | bytes 1179656 | tf_op jit(solution)/shard_map/ppermute | solution.py:230
  19.5 2.2 %collective-permute-start.4 = (f32[2,64,384]{2,1,0:T(8,128)S(1)}, f32[2,64,384]{2,1,0:T(8,128)S(1)}, u32[]{:S(2)}, u32[]{:S(2)}) collective-permute-start(f32[2,64,384]{2,1,0:T(8,128)S(1)} %get-tuple-element.24), channel_id=1, source_target_pairs={{0,8},{1,25},{2,10},{3,27},{4,12},{5,29},{6,14},{7,31},{8,16},{9,1... | collective-permute-start | bytes 589832 | tf_op jit(solution)/shard_map/ppermute | solution.py:230
  21.7 2.2 %collective-permute-start.1 = (f32[2,64,384]{2,1,0:T(8,128)S(1)}, f32[2,64,384]{2,1,0:T(8,128)S(1)}, u32[]{:S(2)}, u32[]{:S(2)}) collective-permute-start(f32[2,64,384]{2,1,0:T(8,128)S(1)} %get-tuple-element.20), channel_id=1, source_target_pairs={{0,4},{1,29},{2,6},{3,31},{4,8},{5,1},{6,10},{7,3},{8,12},{9,5},{1... | collective-permute-start | bytes 589832 | tf_op jit(solution)/shard_map/ppermute | solution.py:230
  23.9 2.4 %collective-permute-start.2 = (f32[2,64,384]{2,1,0:T(8,128)S(1)}, f32[2,64,384]{2,1,0:T(8,128)S(1)}, u32[]{:S(2)}, u32[]{:S(2)}) collective-permute-start(f32[2,64,384]{2,1,0:T(8,128)S(1)} %get-tuple-element.21), channel_id=1, source_target_pairs={{0,5},{1,28},{2,7},{3,30},{4,9},{5,0},{6,11},{7,2},{8,13},{9,4},{1... | collective-permute-start | bytes 589832 | tf_op jit(solution)/shard_map/ppermute | solution.py:230
  26.3 2.2 %collective-permute-done.4.refs_2_ = f32[2,64,384]{2,1,0:T(8,128)S(1)} collective-permute-done((f32[2,64,384]{2,1,0:T(8,128)S(1)}, f32[2,64,384]{2,1,0:T(8,128)S(1)}, u32[]{:S(2)}, u32[]{:S(2)}) %collective-permute-start.4) | collective-permute-done | bytes 196640 | tf_op jit(solution)/shard_map/ppermute | solution.py:230
  28.4 0.0 collective-permute-done.3.refs_1_
  28.4 0.0 copy-start.3
  28.4 0.0 copy-start.2
  28.4 0.0 copy-start.1
  28.5 6.2 %collective-permute-start.5 = (f32[2,64,384]{2,1,0:T(8,128)S(1)}, f32[2,64,384]{2,1,0:T(8,128)S(1)}, u32[]{:S(2)}, u32[]{:S(2)}) collective-permute-start(f32[2,64,384]{2,1,0:T(8,128)S(1)} %shard_map.61), channel_id=1, source_target_pairs={{0,8},{1,25},{2,10},{3,27},{4,12},{5,29},{6,14},{7,31},{8,16},{9,1... | collective-permute-start | bytes 589832 | tf_op jit(solution)/shard_map/ppermute | solution.py:230
  34.7 2.8 %collective-permute-start.6 = (f32[2,64,384]{2,1,0:T(8,128)S(1)}, f32[2,64,384]{2,1,0:T(8,128)S(1)}, u32[]{:S(2)}, u32[]{:S(2)}) collective-permute-start(f32[2,64,384]{2,1,0:T(8,128)S(1)} %shard_map.62), channel_id=1, source_target_pairs={{0,9},{1,24},{2,11},{3,26},{4,13},{5,28},{6,15},{7,30},{8,17},{9,0... | collective-permute-start | bytes 589832 | tf_op jit(solution)/shard_map/ppermute | solution.py:230
  37.5 0.0 collective-permute-done.1.refs_1_
  37.5 0.0 collective-permute-done.2.refs_2_
  37.5 0.4 collective-permute-done.5.refs_3_
  37.9 7.3 %collective-permute-done.6.refs_4_ = f32[2,64,384]{2,1,0:T(8,128)S(1)} collective-permute-done((f32[2,64,384]{2,1,0:T(8,128)S(1)}, f32[2,64,384]{2,1,0:T(8,128)S(1)}, u32[]{:S(2)}, u32[]{:S(2)}) %collective-permute-start.6) | collective-permute-done | bytes 196640 | tf_op jit(solution)/shard_map/ppermute | solution.py:230
  45.3 3.5 %collective-permute-start.7 = (f32[64,384]{1,0:T(8,128)S(1)}, f32[64,384]{1,0:T(8,128)S(1)}, u32[]{:S(2)}, u32[]{:S(2)}) collective-permute-start(f32[64,384]{1,0:T(8,128)S(1)} %get-tuple-element.26), channel_id=1, source_target_pairs={{0,2},{1,3},{2,0},{3,1},{4,6},{5,7},{6,4},{7,5},{8,10},{9,11},{10,... | collective-permute-start | bytes 294920 | tf_op jit(solution)/shard_map/ppermute | solution.py:230
  48.8 0.0 copy-done.3
  48.8 0.1 reshape.21.index_ref
  48.9 0.0 copy-done.2
  48.9 0.4 shard_map.64
  49.3 1.4 %collective-permute-done.7.refs_1_ = f32[64,384]{1,0:T(8,128)S(1)} collective-permute-done((f32[64,384]{1,0:T(8,128)S(1)}, f32[64,384]{1,0:T(8,128)S(1)}, u32[]{:S(2)}, u32[]{:S(2)}) %collective-permute-start.7) | collective-permute-done | bytes 98336 | tf_op jit(solution)/shard_map/ppermute | solution.py:230
  50.8 0.0 copy-done.1
  50.8 1.6 %shard_map.65 = (f32[64,384]{1,0:T(8,128)}, f32[16,8,128]{2,1,0:T(8,128)S(1)}) custom-call(f32[64,384]{1,0:T(8,128)S(1)} %get-tuple-element.25.refs_0_, f32[64,384]{1,0:T(8,128)S(1)} %collective-permute-done.7.refs_1_, f32[64,384]{1,0:T(8,128)S(1)} %bitcast.5, f32[192,64]{1,0:T(8,128)S(1)} %get-tuple-element.27.refs_3_, ...), custom_call_target="tpu_custom_call" | custom-call | tf_op jit(solution)/shard_map/pallas_call | solution.py:191
  52.4 18.7 %all_to_all.5.all_ref = f32[16,8,128]{2,1,0:T(8,128)S(1)} all-to-all(f32[16,8,128]{2,1,0:T(8,128)S(1)} %get-tuple-element.31), channel_id=1, replica_groups=mesh['x'=4,'yh'=4,'z'=8,'yl'=2,'c'=2] {'x','yh'}, dimensions={0} | all-to-all | bytes 131072 | tf_op jit(solution)/shard_map/all_to_all | solution.py:252
  71.1 1.0 %shard_map.66 = f32[64,384]{1,0:T(8,128)} custom-call(f32[16,8,128]{2,1,0:T(8,128)S(1)} %all_to_all.5.all_ref, f32[192,128]{1,0:T(8,128)S(1)} %get-tuple-element.28.refs_4_.cols_ref, f32[64,192]{1,0:T(8,128)S(1)} %get-tuple-element.29.refs_5_.rows_t_ref), custom_call_target="tpu_custom_call" | custom-call | tf_op jit(solution)/shard_map/pallas_call | solution.py:210
  (4 shorter events, 0.1 us)
Async XLA Ops:
  0.6 1.4 %copy-start = (bf16[1,1,1,64,12288]{4,3,2,1,0:T(8,128)(2,1)S(1)}, bf16[1,1,1,64,12288]{4,3,2,1,0:T(8,128)(2,1)}, u32[]{:S(2)}) copy-start(bf16[1,1,1,64,12288]{4,3,2,1,0:T(8,128)(2,1)} %param.4) | copy-start | bytes 4718596
  2.2 11.8 %collective-permute-start = (f32[8,2,64,384]{3,2,1,0:T(8,128)S(1)}, f32[8,2,64,384]{3,2,1,0:T(8,128)S(1)}, u32[]{:S(2)}, u32[]{:S(2)}) collective-permute-start(f32[8,2,64,384]{3,2,1,0:T(8,128)S(1)} %get-tuple-element.18), channel_id=1, source_target_pairs={{0,1},{1,0},{2,3},{3,2},{4,5},{5,4},{6,7},{7,6},{8,9},{9,8},{10,11... | collective-permute-start | bytes 4718600 | tf_op jit(solution)/shard_map/ppermute | solution.py:230
  14.2 14.2 %collective-permute-start.3 = (f32[2,2,64,384]{3,2,1,0:T(8,128)S(1)}, f32[2,2,64,384]{3,2,1,0:T(8,128)S(1)}, u32[]{:S(2)}, u32[]{:S(2)}) collective-permute-start(f32[2,2,64,384]{3,2,1,0:T(8,128)S(1)} %get-tuple-element.23), channel_id=1, source_target_pairs={{0,4},{1,29},{2,6},{3,31},{4,8},{5,1},{6,10},{7,3},{8,12},{9,5},{1... | collective-permute-start | bytes 1179656 | tf_op jit(solution)/shard_map/ppermute | solution.py:230
  19.5 8.9 %collective-permute-start.4 = (f32[2,64,384]{2,1,0:T(8,128)S(1)}, f32[2,64,384]{2,1,0:T(8,128)S(1)}, u32[]{:S(2)}, u32[]{:S(2)}) collective-permute-start(f32[2,64,384]{2,1,0:T(8,128)S(1)} %get-tuple-element.24), channel_id=1, source_target_pairs={{0,8},{1,25},{2,10},{3,27},{4,12},{5,29},{6,14},{7,31},{8,16},{9,1... | collective-permute-start | bytes 589832 | tf_op jit(solution)/shard_map/ppermute | solution.py:230
  21.7 15.8 %collective-permute-start.1 = (f32[2,64,384]{2,1,0:T(8,128)S(1)}, f32[2,64,384]{2,1,0:T(8,128)S(1)}, u32[]{:S(2)}, u32[]{:S(2)}) collective-permute-start(f32[2,64,384]{2,1,0:T(8,128)S(1)} %get-tuple-element.20), channel_id=1, source_target_pairs={{0,4},{1,29},{2,6},{3,31},{4,8},{5,1},{6,10},{7,3},{8,12},{9,5},{1... | collective-permute-start | bytes 589832 | tf_op jit(solution)/shard_map/ppermute | solution.py:230
  23.9 13.6 %collective-permute-start.2 = (f32[2,64,384]{2,1,0:T(8,128)S(1)}, f32[2,64,384]{2,1,0:T(8,128)S(1)}, u32[]{:S(2)}, u32[]{:S(2)}) collective-permute-start(f32[2,64,384]{2,1,0:T(8,128)S(1)} %get-tuple-element.21), channel_id=1, source_target_pairs={{0,5},{1,28},{2,7},{3,30},{4,9},{5,0},{6,11},{7,2},{8,13},{9,4},{1... | collective-permute-start | bytes 589832 | tf_op jit(solution)/shard_map/ppermute | solution.py:230
  28.4 20.4 %copy-start.3 = (s32[1,1,6,32]{3,1,2,0:T(1,128)S(1)}, s32[1,1,6,32]{3,1,2,0:T(1,128)}, u32[]{:S(2)}) copy-start(s32[1,1,6,32]{3,1,2,0:T(1,128)} %param.6) | copy-start | bytes 2308
  28.4 20.5 %copy-start.2 = (f32[64,64]{1,0:T(8,128)S(1)}, f32[64,64]{1,0:T(8,128)}, u32[]{:S(2)}) copy-start(f32[64,64]{1,0:T(8,128)} %constant.2.clone.dct_ref) | copy-start | bytes 49156
  28.4 22.3 %copy-start.1 = (f32[1,1,64,384]{3,2,1,0:T(8,128)S(1)}, f32[1,1,64,384]{3,2,1,0:T(8,128)}, u32[]{:S(2)}) copy-start(f32[1,1,64,384]{3,2,1,0:T(8,128)} %param.5) | copy-start | bytes 294916
  28.5 9.5 %collective-permute-start.5 = (f32[2,64,384]{2,1,0:T(8,128)S(1)}, f32[2,64,384]{2,1,0:T(8,128)S(1)}, u32[]{:S(2)}, u32[]{:S(2)}) collective-permute-start(f32[2,64,384]{2,1,0:T(8,128)S(1)} %shard_map.61), channel_id=1, source_target_pairs={{0,8},{1,25},{2,10},{3,27},{4,12},{5,29},{6,14},{7,31},{8,16},{9,1... | collective-permute-start | bytes 589832 | tf_op jit(solution)/shard_map/ppermute | solution.py:230
  34.7 10.5 %collective-permute-start.6 = (f32[2,64,384]{2,1,0:T(8,128)S(1)}, f32[2,64,384]{2,1,0:T(8,128)S(1)}, u32[]{:S(2)}, u32[]{:S(2)}) collective-permute-start(f32[2,64,384]{2,1,0:T(8,128)S(1)} %shard_map.62), channel_id=1, source_target_pairs={{0,9},{1,24},{2,11},{3,26},{4,13},{5,28},{6,15},{7,30},{8,17},{9,0... | collective-permute-start | bytes 589832 | tf_op jit(solution)/shard_map/ppermute | solution.py:230
  45.3 5.5 %collective-permute-start.7 = (f32[64,384]{1,0:T(8,128)S(1)}, f32[64,384]{1,0:T(8,128)S(1)}, u32[]{:S(2)}, u32[]{:S(2)}) collective-permute-start(f32[64,384]{1,0:T(8,128)S(1)} %get-tuple-element.26), channel_id=1, source_target_pairs={{0,2},{1,3},{2,0},{3,1},{4,6},{5,7},{6,4},{7,5},{8,10},{9,11},{10,... | collective-permute-start | bytes 294920 | tf_op jit(solution)/shard_map/ppermute | solution.py:230

commit v2 on v1

v2 whole, which is shorter than its diff:
```python
import functools

import jax
import jax.numpy as jnp
import numpy as np
from jax import lax
from jax.experimental import pallas as pl
from jax.experimental.pallas import tpu as pltpu
from jax.sharding import Mesh
from jax.sharding import PartitionSpec as P

BLOCK = 64
BETA_DECAY = 0.999
SOFTNESS = 0.02
WIDE = 384
PAIRS = WIDE // 128
KEPT = 64
SIZES = {"x": 4, "yh": 4, "z": 8, "yl": 2, "c": 2}
REP = ("x", "yh")
FSDP = ("z", "yl", "c")
PLACES = (
    [(3, part, side) for part in range(2) for side in range(2)]
    + [(4, 0, side) for side in range(2)]
    + [(k, part, side) for k in (1, 2) for part in range(2) for side in range(2)]
    + [(0, 0, side) for side in range(2)]
)
HIGHEST = lax.Precision.HIGHEST


def dct_matrix():
    k = np.arange(BLOCK)[:, None]
    n = np.arange(BLOCK)[None, :]
    scale = np.where(k == 0, np.sqrt(1.0 / BLOCK), np.sqrt(2.0 / BLOCK))
    return (scale * np.cos(np.pi * (2 * n + 1) * k / (2 * BLOCK))).astype(np.float32)


def dot(a, b, precision=None):
    return jnp.dot(a, b, precision=precision, preferred_element_type=jnp.float32)


def halves(a):
    high = a.astype(jnp.bfloat16)
    return high, (a - high.astype(jnp.float32)).astype(jnp.bfloat16)


def dot_halves(a, b):
    return dot(a[0], b[0]) + (dot(a[1], b[0]) + dot(a[0], b[1]))


def vmem():
    return pl.BlockSpec(memory_space=pltpu.VMEM)


def f32(*shape):
    return jax.ShapeDtypeStruct(shape, jnp.float32)


def bf16(*shape):
    return jax.ShapeDtypeStruct(shape, jnp.bfloat16)


def params():
    return pltpu.CompilerParams(vmem_limit_bytes=32 * 1024 * 1024)


def pick_kernel(other, grads_ref, out_ref):
    z = lax.axis_index("z")
    yl = lax.axis_index("yl")
    core = lax.axis_index("c")
    core = 1 - core if other else core
    for slot, (distance, part, side) in enumerate(PLACES):
        target = lax.rem(z + 8 + (1 - 2 * core) * distance, 8)
        block = 4 * target + 2 * (1 - yl if side else yl) + (1 - core if part else core)
        start = pl.multiple_of(block * WIDE, 128)
        out_ref[slot] = grads_ref[:, pl.ds(start, WIDE)].astype(jnp.float32)


def pick(grads, other):
    return pl.pallas_call(
        functools.partial(pick_kernel, other),
        out_shape=f32(len(PLACES), BLOCK, WIDE),
        in_specs=[vmem()],
        out_specs=vmem(),
        compiler_params=params(),
    )(grads)


def table_kernel(index_ref, dct_ref, u_ref, u_high_ref, u_low_ref, v_t_ref, v_high_ref, v_low_ref):
    dct = dct_ref[...]
    index = index_ref[...]
    size = index.shape[-1]
    iota = lax.broadcasted_iota(jnp.int32, (BLOCK, size), 0)
    hot_u = (iota == lax.shift_right_logical(index, 6)).astype(jnp.float32)
    hot_v = (iota == jnp.bitwise_and(index, 63)).astype(jnp.float32)
    twice = jnp.concatenate([dct, dct], axis=1)
    lane = lax.broadcasted_iota(jnp.int32, (size, 128), 1)
    kept = lax.broadcasted_iota(jnp.int32, (size, 128), 0)
    mine = jnp.bitwise_and(lax.shift_right_logical(kept, 5), 1) == lax.shift_right_logical(lane, 6)
    u = dot(dct.T, hot_u, HIGHEST)
    v = jnp.where(mine, dot(hot_v.T, twice, HIGHEST), 0.0)
    for p in range(PAIRS):
        span = slice(p * KEPT, (p + 1) * KEPT)
        u_ref[p] = u[:, span]
        u_high_ref[p], u_low_ref[p] = halves(u[:, span])
        v_t_ref[p] = v[span].T
        v_high_ref[p], v_low_ref[p] = halves(v[span])


def tables(index):
    square, wide = (PAIRS, BLOCK, KEPT), (PAIRS, KEPT, 128)
    return pl.pallas_call(
        table_kernel,
        out_shape=(f32(*square), bf16(*square), bf16(*square), f32(PAIRS, 128, KEPT), bf16(*wide), bf16(*wide)),
        in_specs=[vmem()] * 2,
        out_specs=(vmem(),) * 6,
        compiler_params=params(),
    )(index, dct_matrix())


def sums_kernel(plan, *refs):
    ins, outs = refs[: len(refs) - len(plan)], refs[len(refs) - len(plan) :]
    for out, rows in zip(outs, plan):
        for row, terms in enumerate(rows):
            out[row] = functools.reduce(jnp.add, [ins[i][j] for i, j in terms])


def sums(plan, *arrays):
    return pl.pallas_call(
        functools.partial(sums_kernel, plan),
        out_shape=tuple(f32(len(rows), BLOCK, WIDE) for rows in plan),
        in_specs=[vmem()] * len(arrays),
        out_specs=(vmem(),) * len(plan),
        compiler_params=params(),
    )(*arrays)


def extract_kernel(*refs):
    *terms, momentum_ref, u_high_ref, u_low_ref, v_t_ref, updated_ref, own_ref, kept_ref = refs
    updated = functools.reduce(jnp.add, [r[0] for r in terms]) + BETA_DECAY * momentum_ref[...]
    updated_ref[...] = updated
    columns = updated.T
    row = lax.broadcasted_iota(jnp.int32, (8, KEPT), 0)
    tile = jnp.zeros((8, KEPT), jnp.float32)
    for p in range(PAIRS):
        field = halves(columns[p * 128 : (p + 1) * 128])
        product = dot_halves(field, (u_high_ref[p], u_low_ref[p])) * v_t_ref[p]
        tile = jnp.where(row == p, jnp.sum(product, axis=0, keepdims=True), tile)
    tile = jnp.concatenate([tile, jnp.zeros((8, 128 - KEPT), jnp.float32)], axis=1)
    own_ref[...] = tile
    for r in range(kept_ref.shape[0]):
        kept_ref[r] = tile


def extract(groups, *args):
    return pl.pallas_call(
        extract_kernel,
        out_shape=(f32(BLOCK, WIDE), f32(8, 128), f32(groups, 8, 128)),
        in_specs=[vmem()] * len(args),
        out_specs=(vmem(),) * 3,
        compiler_params=params(),
    )(*args)


def finish_kernel(updated_ref, own_ref, all_ref, u_ref, v_high_ref, v_low_ref, new_ref, update_ref):
    averaged = jnp.sum(all_ref[...], axis=0) * (1.0 / all_ref.shape[0])
    own = own_ref[...]
    for p in range(PAIRS):
        span = slice(p * 128, (p + 1) * 128)
        v = (v_high_ref[p], v_low_ref[p])
        inverse = lambda kept: dot_halves(halves(u_ref[p] * kept[p : p + 1, :KEPT]), v)
        direction = inverse(averaged)
        update_ref[:, span] = direction * lax.rsqrt(direction * direction + SOFTNESS * SOFTNESS)
        new_ref[:, span] = updated_ref[:, span] - inverse(own)


def finish(*args):
    return pl.pallas_call(
        finish_kernel,
        out_shape=(f32(BLOCK, WIDE),) * 2,
        in_specs=[vmem()] * len(args),
        out_specs=(vmem(),) * 2,
        compiler_params=params(),
    )(*args)


def permutation(hops, flip_yl, flip_c):
    flat = lambda z, yl, c: (z % 8) * 4 + yl * 2 + c
    return [
        (flat(z, yl, c), flat(z + hops * (1 - 2 * c), yl ^ flip_yl, c ^ flip_c))
        for z in range(8)
        for yl in range(2)
        for c in range(2)
    ]


def send(array, hops=0, yl=0, c=0):
    return lax.ppermute(array, FSDP, permutation(hops, yl, c))


def per_device(partial_grads, momentum, keep_index):
    grads = partial_grads.reshape(BLOCK, -1)
    momentum = momentum.reshape(BLOCK, WIDE)

    got = send(pick(grads, True), c=1)
    own = pick(grads, False)
    u, u_high, u_low, v_t, v_high, v_low = tables(keep_index.reshape(1, -1))
    join = lambda *slots: [[(0, i), (1, i)] for i in slots]
    three, four, near, near_x, two, here = sums(
        [join(0, 1, 2, 3), join(4, 5), join(6, 7), join(8, 9), join(10, 11, 12, 13), join(14, 15)], own, got
    )
    three = send(three, hops=1)
    four = send(four, hops=2)
    near = send(near, hops=1)
    near_x = send(near_x, hops=1, c=1)
    (far_x,) = sums([[[(0, 2 + s), (1, 2 + s)] for s in range(2)]], two, three, four)
    far_x = send(far_x, hops=2, c=1)
    far, far_y = sums([[[(0, s), (1, s), (2, s)]] for s in range(2)], two, three, four)
    far = send(far, hops=2)
    far_y = send(far_y, hops=2, yl=1)
    mine, other = sums([[[(i, s) for i in range(4)]] for s in range(2)], here, near, near_x, far_x)
    other = send(other, yl=1)

    groups = SIZES["x"] * SIZES["yh"]
    updated, kept, to_all = extract(groups, mine, other, far, far_y, momentum, u_high, u_low, v_t)
    from_all = lax.all_to_all(to_all, REP, 0, 0, tiled=True)
    new_momentum, update = finish(updated, kept, from_all, u, v_high, v_low)
    return new_momentum.reshape(1, 1, BLOCK, WIDE), update.reshape(1, BLOCK, WIDE)


def solution(mesh):
    inner = Mesh(mesh.devices.reshape(tuple(SIZES.values())), tuple(SIZES))
    in_specs = (
        P(REP, FSDP, None, None, None),
        P(REP, None, None, FSDP),
        P(None, None, FSDP, None),
    )
    out_specs = (P(REP, None, None, FSDP), P(None, None, FSDP))
    return jax.shard_map(
        per_device, mesh=inner, in_specs=in_specs, out_specs=out_specs, check_vma=False
    )
```

time: 72.5 us -> 68 us (0.938)
  the two profiles are of different devices: /device:TPU:1 before, /device:TPU:8 now
where the time goes in v2:
time: 68 us; the launch traced here: 67.6 us
  starting transfers between devices  33 us (49%)
  blocking collectives  19.2 us (28%)
  waiting for transfers between devices  10.9 us (16%)
  Pallas kernels  2.15 us (3%)
  local copies, waits for them, and re-layouts  1.5 us (2%)
  between operations  0.81 us (1%)
    ppermute x9, starting transfers between devices, send(): return lax.ppermute(array, FSDP, permutation(hops, yl, c))  33 us
    all_to_all x1, blocking collectives, per_device(): from_all = lax.all_to_all(to_all, REP, 0, 0, tiled=True)  19.2 us
    ppermute x9, waiting for transfers between devices, send(): return lax.ppermute(array, FSDP, permutation(hops, yl, c))  10.9 us
    unnamed x8, local copies, waits for them, and re-layouts  1.42 us
  transfers between devices with their start and end apart: 9, of which 5 were waited for; matrix products, arithmetic and copies ran while one was open for 0% of the time, Pallas kernels for 1%

profile of v2, /device:TPU:8, one launch (start us, length us, event | category | flops | bytes accessed | tf_op | source)
XLA Modules:
  0.0 67.6 jit_solution(13033079178523092227)
XLA Ops:
  0.6 0.0 copy-start
  0.6 1.4 %copy-done = bf16[1,1,1,64,12288]{4,3,2,1,0:T(8,128)(2,1)S(1)} copy-done((bf16[1,1,1,64,12288]{4,3,2,1,0:T(8,128)(2,1)S(1)}, bf16[1,1,1,64,12288]{4,3,2,1,0:T(8,128)(2,1)}, u32[]{:S(2)}) %copy-start) | copy-done | bytes 1572888
  2.0 0.1 shard_map.60
  2.1 1.9 %collective-permute-start = (f32[16,64,384]{2,1,0:T(8,128)S(1)}, f32[16,64,384]{2,1,0:T(8,128)S(1)}, u32[]{:S(2)}, u32[]{:S(2)}) collective-permute-start(f32[16,64,384]{2,1,0:T(8,128)S(1)} %shard_map.60), channel_id=1, source_target_pairs={{0,1},{1,0},{2,3},{3,2},{4,5},{5,4},{6,7},{7,6},{8,9},{9,8},{10,11... | collective-permute-start | bytes 4718600 | tf_op jit(solution)/shard_map/ppermute | solution.py:197
  4.1 0.1 shard_map.59.refs_0_
  4.2 3.2 %collective-permute-done.refs_1_ = f32[16,64,384]{2,1,0:T(8,128)S(1)} collective-permute-done((f32[16,64,384]{2,1,0:T(8,128)S(1)}, f32[16,64,384]{2,1,0:T(8,128)S(1)}, u32[]{:S(2)}, u32[]{:S(2)}) %collective-permute-start) | collective-permute-done | bytes 1572896 | tf_op jit(solution)/shard_map/ppermute | solution.py:197
  7.4 0.2 shard_map.61
  7.6 0.0 copy-start.3
  7.6 0.0 copy-start.2
  7.6 0.0 copy-start.1
  7.6 4.4 %collective-permute-start.3 = (f32[4,64,384]{2,1,0:T(8,128)S(1)}, f32[4,64,384]{2,1,0:T(8,128)S(1)}, u32[]{:S(2)}, u32[]{:S(2)}) collective-permute-start(f32[4,64,384]{2,1,0:T(8,128)S(1)} %get-tuple-element.27), channel_id=1, source_target_pairs={{0,4},{1,29},{2,6},{3,31},{4,8},{5,1},{6,10},{7,3},{8,12},{9,5},{1... | collective-permute-start | bytes 1179656 | tf_op jit(solution)/shard_map/ppermute | solution.py:197
  12.1 6.1 %collective-permute-start.4 = (f32[2,64,384]{2,1,0:T(8,128)S(1)}, f32[2,64,384]{2,1,0:T(8,128)S(1)}, u32[]{:S(2)}, u32[]{:S(2)}) collective-permute-start(f32[2,64,384]{2,1,0:T(8,128)S(1)} %get-tuple-element.28), channel_id=1, source_target_pairs={{0,8},{1,25},{2,10},{3,27},{4,12},{5,29},{6,14},{7,31},{8,16},{9,1... | collective-permute-start | bytes 589832 | tf_op jit(solution)/shard_map/ppermute | solution.py:197
  18.2 5.5 %collective-permute-start.1 = (f32[2,64,384]{2,1,0:T(8,128)S(1)}, f32[2,64,384]{2,1,0:T(8,128)S(1)}, u32[]{:S(2)}, u32[]{:S(2)}) collective-permute-start(f32[2,64,384]{2,1,0:T(8,128)S(1)} %get-tuple-element.24), channel_id=1, source_target_pairs={{0,4},{1,29},{2,6},{3,31},{4,8},{5,1},{6,10},{7,3},{8,12},{9,5},{1... | collective-permute-start | bytes 589832 | tf_op jit(solution)/shard_map/ppermute | solution.py:197
  23.7 2.3 %collective-permute-start.2 = (f32[2,64,384]{2,1,0:T(8,128)S(1)}, f32[2,64,384]{2,1,0:T(8,128)S(1)}, u32[]{:S(2)}, u32[]{:S(2)}) collective-permute-start(f32[2,64,384]{2,1,0:T(8,128)S(1)} %get-tuple-element.25), channel_id=1, source_target_pairs={{0,5},{1,28},{2,7},{3,30},{4,9},{5,0},{6,11},{7,2},{8,13},{9,4},{1... | collective-permute-start | bytes 589832 | tf_op jit(solution)/shard_map/ppermute | solution.py:197
  26.0 4.3 %collective-permute-done.4.refs_2_ = f32[2,64,384]{2,1,0:T(8,128)S(1)} collective-permute-done((f32[2,64,384]{2,1,0:T(8,128)S(1)}, f32[2,64,384]{2,1,0:T(8,128)S(1)}, u32[]{:S(2)}, u32[]{:S(2)}) %collective-permute-start.4) | collective-permute-done | bytes 196640 | tf_op jit(solution)/shard_map/ppermute | solution.py:197
  30.2 0.0 collective-permute-done.3.refs_1_
  30.3 1.9 %collective-permute-start.5 = (f32[2,64,384]{2,1,0:T(8,128)S(1)}, f32[2,64,384]{2,1,0:T(8,128)S(1)}, u32[]{:S(2)}, u32[]{:S(2)}) collective-permute-start(f32[2,64,384]{2,1,0:T(8,128)S(1)} %shard_map.62), channel_id=1, source_target_pairs={{0,9},{1,24},{2,11},{3,26},{4,13},{5,28},{6,15},{7,30},{8,17},{9,0... | collective-permute-start | bytes 589832 | tf_op jit(solution)/shard_map/ppermute | solution.py:197
  32.2 3.5 %collective-permute-start.7 = (f32[1,64,384]{2,1,0:T(8,128)S(1)}, f32[1,64,384]{2,1,0:T(8,128)S(1)}, u32[]{:S(2)}, u32[]{:S(2)}) collective-permute-start(f32[1,64,384]{2,1,0:T(8,128)S(1)} %get-tuple-element.31), channel_id=1, source_target_pairs={{0,8},{1,25},{2,10},{3,27},{4,12},{5,29},{6,14},{7,31},{8,16},{9,1... | collective-permute-start | bytes 294920 | tf_op jit(solution)/shard_map/ppermute | solution.py:197
  35.8 4.4 %collective-permute-start.8 = (f32[1,64,384]{2,1,0:T(8,128)S(1)}, f32[1,64,384]{2,1,0:T(8,128)S(1)}, u32[]{:S(2)}, u32[]{:S(2)}) collective-permute-start(f32[1,64,384]{2,1,0:T(8,128)S(1)} %get-tuple-element.32), channel_id=1, source_target_pairs={{0,10},{1,27},{2,8},{3,25},{4,14},{5,31},{6,12},{7,29},{8,18},{9,3... | collective-permute-start | bytes 294920 | tf_op jit(solution)/shard_map/ppermute | solution.py:197
  40.1 0.0 collective-permute-done.1.refs_1_
  40.2 0.0 collective-permute-done.2.refs_2_
  40.2 0.5 collective-permute-done.5.refs_3_
  40.7 3.0 %collective-permute-start.6 = (f32[1,64,384]{2,1,0:T(8,128)S(1)}, f32[1,64,384]{2,1,0:T(8,128)S(1)}, u32[]{:S(2)}, u32[]{:S(2)}) collective-permute-start(f32[1,64,384]{2,1,0:T(8,128)S(1)} %get-tuple-element.30), channel_id=1, source_target_pairs={{0,2},{1,3},{2,0},{3,1},{4,6},{5,7},{6,4},{7,5},{8,10},{9,11},{10,... | collective-permute-start | bytes 294920 | tf_op jit(solution)/shard_map/ppermute | solution.py:197
  43.7 0.0 copy-done.3
  43.7 0.1 reshape.21.index_ref
  43.8 0.0 copy-done.2
  43.8 0.5 shard_map.65
  44.3 0.0 collective-permute-done.7.refs_2_
  44.3 1.8 %collective-permute-done.8.refs_3_ = f32[1,64,384]{2,1,0:T(8,128)S(1)} collective-permute-done((f32[1,64,384]{2,1,0:T(8,128)S(1)}, f32[1,64,384]{2,1,0:T(8,128)S(1)}, u32[]{:S(2)}, u32[]{:S(2)}) %collective-permute-start.8) | collective-permute-done | bytes 98336 | tf_op jit(solution)/shard_map/ppermute | solution.py:197
  46.1 1.0 %collective-permute-done.6.refs_1_ = f32[1,64,384]{2,1,0:T(8,128)S(1)} collective-permute-done((f32[1,64,384]{2,1,0:T(8,128)S(1)}, f32[1,64,384]{2,1,0:T(8,128)S(1)}, u32[]{:S(2)}, u32[]{:S(2)}) %collective-permute-start.6) | collective-permute-done | bytes 98336 | tf_op jit(solution)/shard_map/ppermute | solution.py:197
  47.2 0.0 copy-done.1
  47.2 0.3 shard_map.66
  47.5 19.2 %all_to_all.5.all_ref = f32[16,8,128]{2,1,0:T(8,128)S(1)} all-to-all(f32[16,8,128]{2,1,0:T(8,128)S(1)} %get-tuple-element.38), channel_id=1, replica_groups=mesh['x'=4,'yh'=4,'z'=8,'yl'=2,'c'=2] {'x','yh'}, dimensions={0} | all-to-all | bytes 131072 | tf_op jit(solution)/shard_map/all_to_all | solution.py:225
  66.7 0.9 %shard_map.67 = (f32[64,384]{1,0:T(8,128)}, f32[64,384]{1,0:T(8,128)}) custom-call(f32[64,384]{1,0:T(8,128)S(1)} %get-tuple-element.36.updated_ref, f32[8,128]{1,0:T(8,128)S(1)} %get-tuple-element.37.own_ref, f32[16,8,128]{2,1,0:T(8,128)S(1)} %all_to_all.5.all_ref, f32[3,64,64]{2,1,0:T(8,128)S(1)} %get-tuple-element.39.u_ref, ...), custom_call_target="tpu_custom_call" | custom-call | tf_op jit(solution)/shard_map/pallas_call | solution.py:177
  (4 shorter events, 0.1 us)
Async XLA Ops:
  0.6 1.4 %copy-start = (bf16[1,1,1,64,12288]{4,3,2,1,0:T(8,128)(2,1)S(1)}, bf16[1,1,1,64,12288]{4,3,2,1,0:T(8,128)(2,1)}, u32[]{:S(2)}) copy-start(bf16[1,1,1,64,12288]{4,3,2,1,0:T(8,128)(2,1)} %param.4) | copy-start | bytes 4718596
  2.1 5.3 %collective-permute-start = (f32[16,64,384]{2,1,0:T(8,128)S(1)}, f32[16,64,384]{2,1,0:T(8,128)S(1)}, u32[]{:S(2)}, u32[]{:S(2)}) collective-permute-start(f32[16,64,384]{2,1,0:T(8,128)S(1)} %shard_map.60), channel_id=1, source_target_pairs={{0,1},{1,0},{2,3},{3,2},{4,5},{5,4},{6,7},{7,6},{8,9},{9,8},{10,11... | collective-permute-start | bytes 4718600 | tf_op jit(solution)/shard_map/ppermute | solution.py:197
  7.6 36.1 %copy-start.3 = (s32[1,1,6,32]{3,1,2,0:T(1,128)S(1)}, s32[1,1,6,32]{3,1,2,0:T(1,128)}, u32[]{:S(2)}) copy-start(s32[1,1,6,32]{3,1,2,0:T(1,128)} %param.6) | copy-start | bytes 2308
  7.6 36.2 %copy-start.2 = (f32[64,64]{1,0:T(8,128)S(1)}, f32[64,64]{1,0:T(8,128)}, u32[]{:S(2)}) copy-start(f32[64,64]{1,0:T(8,128)} %constant.2.clone.dct_ref) | copy-start | bytes 49156
  7.6 39.5 %copy-start.1 = (f32[1,1,64,384]{3,2,1,0:T(8,128)S(1)}, f32[1,1,64,384]{3,2,1,0:T(8,128)}, u32[]{:S(2)}) copy-start(f32[1,1,64,384]{3,2,1,0:T(8,128)} %param.5) | copy-start | bytes 294916
  7.6 22.6 %collective-permute-start.3 = (f32[4,64,384]{2,1,0:T(8,128)S(1)}, f32[4,64,384]{2,1,0:T(8,128)S(1)}, u32[]{:S(2)}, u32[]{:S(2)}) collective-permute-start(f32[4,64,384]{2,1,0:T(8,128)S(1)} %get-tuple-element.27), channel_id=1, source_target_pairs={{0,4},{1,29},{2,6},{3,31},{4,8},{5,1},{6,10},{7,3},{8,12},{9,5},{1... | collective-permute-start | bytes 1179656 | tf_op jit(solution)/shard_map/ppermute | solution.py:197
  12.1 18.2 %collective-permute-start.4 = (f32[2,64,384]{2,1,0:T(8,128)S(1)}, f32[2,64,384]{2,1,0:T(8,128)S(1)}, u32[]{:S(2)}, u32[]{:S(2)}) collective-permute-start(f32[2,64,384]{2,1,0:T(8,128)S(1)} %get-tuple-element.28), channel_id=1, source_target_pairs={{0,8},{1,25},{2,10},{3,27},{4,12},{5,29},{6,14},{7,31},{8,16},{9,1... | collective-permute-start | bytes 589832 | tf_op jit(solution)/shard_map/ppermute | solution.py:197
  18.2 22.0 %collective-permute-start.1 = (f32[2,64,384]{2,1,0:T(8,128)S(1)}, f32[2,64,384]{2,1,0:T(8,128)S(1)}, u32[]{:S(2)}, u32[]{:S(2)}) collective-permute-start(f32[2,64,384]{2,1,0:T(8,128)S(1)} %get-tuple-element.24), channel_id=1, source_target_pairs={{0,4},{1,29},{2,6},{3,31},{4,8},{5,1},{6,10},{7,3},{8,12},{9,5},{1... | collective-permute-start | bytes 589832 | tf_op jit(solution)/shard_map/ppermute | solution.py:197
  23.7 16.5 %collective-permute-start.2 = (f32[2,64,384]{2,1,0:T(8,128)S(1)}, f32[2,64,384]{2,1,0:T(8,128)S(1)}, u32[]{:S(2)}, u32[]{:S(2)}) collective-permute-start(f32[2,64,384]{2,1,0:T(8,128)S(1)} %get-tuple-element.25), channel_id=1, source_target_pairs={{0,5},{1,28},{2,7},{3,30},{4,9},{5,0},{6,11},{7,2},{8,13},{9,4},{1... | collective-permute-start | bytes 589832 | tf_op jit(solution)/shard_map/ppermute | solution.py:197
  30.3 10.3 %collective-permute-start.5 = (f32[2,64,384]{2,1,0:T(8,128)S(1)}, f32[2,64,384]{2,1,0:T(8,128)S(1)}, u32[]{:S(2)}, u32[]{:S(2)}) collective-permute-start(f32[2,64,384]{2,1,0:T(8,128)S(1)} %shard_map.62), channel_id=1, source_target_pairs={{0,9},{1,24},{2,11},{3,26},{4,13},{5,28},{6,15},{7,30},{8,17},{9,0... | collective-permute-start | bytes 589832 | tf_op jit(solution)/shard_map/ppermute | solution.py:197
  32.2 12.1 %collective-permute-start.7 = (f32[1,64,384]{2,1,0:T(8,128)S(1)}, f32[1,64,384]{2,1,0:T(8,128)S(1)}, u32[]{:S(2)}, u32[]{:S(2)}) collective-permute-start(f32[1,64,384]{2,1,0:T(8,128)S(1)} %get-tuple-element.31), channel_id=1, source_target_pairs={{0,8},{1,25},{2,10},{3,27},{4,12},{5,29},{6,14},{7,31},{8,16},{9,1... | collective-permute-start | bytes 294920 | tf_op jit(solution)/shard_map/ppermute | solution.py:197
  35.8 10.4 %collective-permute-start.8 = (f32[1,64,384]{2,1,0:T(8,128)S(1)}, f32[1,64,384]{2,1,0:T(8,128)S(1)}, u32[]{:S(2)}, u32[]{:S(2)}) collective-permute-start(f32[1,64,384]{2,1,0:T(8,128)S(1)} %get-tuple-element.32), channel_id=1, source_target_pairs={{0,10},{1,27},{2,8},{3,25},{4,14},{5,31},{6,12},{7,29},{8,18},{9,3... | collective-permute-start | bytes 294920 | tf_op jit(solution)/shard_map/ppermute | solution.py:197
  40.7 6.5 %collective-permute-start.6 = (f32[1,64,384]{2,1,0:T(8,128)S(1)}, f32[1,64,384]{2,1,0:T(8,128)S(1)}, u32[]{:S(2)}, u32[]{:S(2)}) collective-permute-start(f32[1,64,384]{2,1,0:T(8,128)S(1)} %get-tuple-element.30), channel_id=1, source_target_pairs={{0,2},{1,3},{2,0},{3,1},{4,6},{5,7},{6,4},{7,5},{8,10},{9,11},{10,... | collective-permute-start | bytes 294920 | tf_op jit(solution)/shard_map/ppermute | solution.py:197

commit v3 on v2

--- a/solution.py
+++ b/solution.py
@@ -124,13 +124,14 @@
             out[row] = functools.reduce(jnp.add, [ins[i][j] for i, j in terms])
 
 
-def sums(plan, *arrays):
+def sums(plan, *arrays, weight=0):
     return pl.pallas_call(
         functools.partial(sums_kernel, plan),
         out_shape=tuple(f32(len(rows), BLOCK, WIDE) for rows in plan),
         in_specs=[vmem()] * len(arrays),
         out_specs=(vmem(),) * len(plan),
         compiler_params=params(),
+        cost_estimate=pl.CostEstimate(flops=0, bytes_accessed=int(weight * 3.69e6) or 1, transcendentals=0),
     )(*arrays)
 
 
@@ -212,7 +213,7 @@
     four = send(four, hops=2)
     near = send(near, hops=1)
     near_x = send(near_x, hops=1, c=1)
-    (far_x,) = sums([[[(0, 2 + s), (1, 2 + s)] for s in range(2)]], two, three, four)
+    (far_x,) = sums([[[(0, 2 + s), (1, 2 + s)] for s in range(2)]], two, three)
     far_x = send(far_x, hops=2, c=1)
     far, far_y = sums([[[(0, s), (1, s), (2, s)]] for s in range(2)], two, three, four)
     far = send(far, hops=2)

time: 68 us -> 66.2 us (0.974)
  waiting for transfers between devices: 10.9 us -> 7.4 us
  starting transfers between devices: 33 us -> 35.1 us
    ppermute x9, waiting for transfers between devices: 10.9 us -> 7.4 us  [send(): return lax.ppermute(array, FSDP, permutation(hops, yl, c))]
    ppermute x9, starting transfers between devices: 33 us -> 35.1 us  [send(): return lax.ppermute(array, FSDP, permutation(hops, yl, c))]
  transfers between devices with their start and end apart: 9 -> 9, of which waited for: 5 -> 3; matrix products, arithmetic and copies ran while one was open for 0% -> 0% of each run, Pallas kernels for 1% -> 1%
where the time goes in v3:
time: 66.2 us; the launch traced here: 65.8 us
  starting transfers between devices  35.1 us (53%)
  blocking collectives  18.7 us (28%)
  waiting for transfers between devices  7.4 us (11%)
  Pallas kernels  2.15 us (3%)
  local copies, waits for them, and re-layouts  1.5 us (2%)
  between operations  0.83 us (1%)
    ppermute x9, starting transfers between devices, send(): return lax.ppermute(array, FSDP, permutation(hops, yl, c))  35.1 us
    all_to_all x1, blocking collectives, per_device(): from_all = lax.all_to_all(to_all, REP, 0, 0, tiled=True)  18.7 us
    ppermute x9, waiting for transfers between devices, send(): return lax.ppermute(array, FSDP, permutation(hops, yl, c))  7.4 us
    unnamed x8, local copies, waits for them, and re-layouts  1.42 us
  transfers between devices with their start and end apart: 9, of which 3 were waited for; matrix products, arithmetic and copies ran while one was open for 0% of the time, Pallas kernels for 1%

profile of v3, /device:TPU:8, one launch (start us, length us, event | category | flops | bytes accessed | tf_op | source)
XLA Modules:
  0.0 65.8 jit_solution(7068041609649554069)
XLA Ops:
  0.6 0.0 copy-start
  0.6 1.4 %copy-done = bf16[1,1,1,64,12288]{4,3,2,1,0:T(8,128)(2,1)S(1)} copy-done((bf16[1,1,1,64,12288]{4,3,2,1,0:T(8,128)(2,1)S(1)}, bf16[1,1,1,64,12288]{4,3,2,1,0:T(8,128)(2,1)}, u32[]{:S(2)}) %copy-start) | copy-done | bytes 1572888
  2.0 0.1 shard_map.60
  2.1 1.9 %collective-permute-start = (f32[16,64,384]{2,1,0:T(8,128)S(1)}, f32[16,64,384]{2,1,0:T(8,128)S(1)}, u32[]{:S(2)}, u32[]{:S(2)}) collective-permute-start(f32[16,64,384]{2,1,0:T(8,128)S(1)} %shard_map.60), channel_id=1, source_target_pairs={{0,1},{1,0},{2,3},{3,2},{4,5},{5,4},{6,7},{7,6},{8,9},{9,8},{10,11... | collective-permute-start | bytes 4718600 | tf_op jit(solution)/shard_map/ppermute | solution.py:198
  4.1 0.1 shard_map.59.refs_0_
  4.2 3.2 %collective-permute-done.refs_1_ = f32[16,64,384]{2,1,0:T(8,128)S(1)} collective-permute-done((f32[16,64,384]{2,1,0:T(8,128)S(1)}, f32[16,64,384]{2,1,0:T(8,128)S(1)}, u32[]{:S(2)}, u32[]{:S(2)}) %collective-permute-start) | collective-permute-done | bytes 1572896 | tf_op jit(solution)/shard_map/ppermute | solution.py:198
  7.4 0.2 shard_map.61
  7.6 0.0 copy-start.3
  7.6 0.0 copy-start.2
  7.6 0.0 copy-start.1
  7.6 4.4 %collective-permute-start.3 = (f32[4,64,384]{2,1,0:T(8,128)S(1)}, f32[4,64,384]{2,1,0:T(8,128)S(1)}, u32[]{:S(2)}, u32[]{:S(2)}) collective-permute-start(f32[4,64,384]{2,1,0:T(8,128)S(1)} %get-tuple-element.27), channel_id=1, source_target_pairs={{0,4},{1,29},{2,6},{3,31},{4,8},{5,1},{6,10},{7,3},{8,12},{9,5},{1... | collective-permute-start | bytes 1179656 | tf_op jit(solution)/shard_map/ppermute | solution.py:198
  12.1 6.1 %collective-permute-start.6 = (f32[2,64,384]{2,1,0:T(8,128)S(1)}, f32[2,64,384]{2,1,0:T(8,128)S(1)}, u32[]{:S(2)}, u32[]{:S(2)}) collective-permute-start(f32[2,64,384]{2,1,0:T(8,128)S(1)} %get-tuple-element.30), channel_id=1, source_target_pairs={{0,8},{1,25},{2,10},{3,27},{4,12},{5,29},{6,14},{7,31},{8,16},{9,1... | collective-permute-start | bytes 589832 | tf_op jit(solution)/shard_map/ppermute | solution.py:198
  18.2 5.5 %collective-permute-start.1 = (f32[2,64,384]{2,1,0:T(8,128)S(1)}, f32[2,64,384]{2,1,0:T(8,128)S(1)}, u32[]{:S(2)}, u32[]{:S(2)}) collective-permute-start(f32[2,64,384]{2,1,0:T(8,128)S(1)} %get-tuple-element.24), channel_id=1, source_target_pairs={{0,4},{1,29},{2,6},{3,31},{4,8},{5,1},{6,10},{7,3},{8,12},{9,5},{1... | collective-permute-start | bytes 589832 | tf_op jit(solution)/shard_map/ppermute | solution.py:198
  23.7 2.3 %collective-permute-start.2 = (f32[2,64,384]{2,1,0:T(8,128)S(1)}, f32[2,64,384]{2,1,0:T(8,128)S(1)}, u32[]{:S(2)}, u32[]{:S(2)}) collective-permute-start(f32[2,64,384]{2,1,0:T(8,128)S(1)} %get-tuple-element.25), channel_id=1, source_target_pairs={{0,5},{1,28},{2,7},{3,30},{4,9},{5,0},{6,11},{7,2},{8,13},{9,4},{1... | collective-permute-start | bytes 589832 | tf_op jit(solution)/shard_map/ppermute | solution.py:198
  26.0 0.0 collective-permute-done.3.refs_1_
  26.0 4.2 %collective-permute-start.4 = (f32[2,64,384]{2,1,0:T(8,128)S(1)}, f32[2,64,384]{2,1,0:T(8,128)S(1)}, u32[]{:S(2)}, u32[]{:S(2)}) collective-permute-start(f32[2,64,384]{2,1,0:T(8,128)S(1)} %shard_map.62), channel_id=1, source_target_pairs={{0,9},{1,24},{2,11},{3,26},{4,13},{5,28},{6,15},{7,30},{8,17},{9,0... | collective-permute-start | bytes 589832 | tf_op jit(solution)/shard_map/ppermute | solution.py:198
  30.2 0.1 collective-permute-done.6.refs_2_
  30.3 5.5 %collective-permute-start.7 = (f32[1,64,384]{2,1,0:T(8,128)S(1)}, f32[1,64,384]{2,1,0:T(8,128)S(1)}, u32[]{:S(2)}, u32[]{:S(2)}) collective-permute-start(f32[1,64,384]{2,1,0:T(8,128)S(1)} %get-tuple-element.31), channel_id=1, source_target_pairs={{0,8},{1,25},{2,10},{3,27},{4,12},{5,29},{6,14},{7,31},{8,16},{9,1... | collective-permute-start | bytes 294920 | tf_op jit(solution)/shard_map/ppermute | solution.py:198
  35.8 1.9 %collective-permute-start.8 = (f32[1,64,384]{2,1,0:T(8,128)S(1)}, f32[1,64,384]{2,1,0:T(8,128)S(1)}, u32[]{:S(2)}, u32[]{:S(2)}) collective-permute-start(f32[1,64,384]{2,1,0:T(8,128)S(1)} %get-tuple-element.32), channel_id=1, source_target_pairs={{0,10},{1,27},{2,8},{3,25},{4,14},{5,31},{6,12},{7,29},{8,18},{9,3... | collective-permute-start | bytes 294920 | tf_op jit(solution)/shard_map/ppermute | solution.py:198
  37.7 0.0 collective-permute-done.1.refs_1_
  37.7 0.0 collective-permute-done.2.refs_2_
  37.7 0.0 collective-permute-done.4.refs_3_
  37.8 3.4 %collective-permute-start.5 = (f32[1,64,384]{2,1,0:T(8,128)S(1)}, f32[1,64,384]{2,1,0:T(8,128)S(1)}, u32[]{:S(2)}, u32[]{:S(2)}) collective-permute-start(f32[1,64,384]{2,1,0:T(8,128)S(1)} %get-tuple-element.29), channel_id=1, source_target_pairs={{0,2},{1,3},{2,0},{3,1},{4,6},{5,7},{6,4},{7,5},{8,10},{9,11},{10,... | collective-permute-start | bytes 294920 | tf_op jit(solution)/shard_map/ppermute | solution.py:198
  41.1 0.0 copy-done.3
  41.2 0.1 reshape.21.index_ref
  41.3 0.0 copy-done.2
  41.3 0.5 shard_map.65
  41.7 0.0 collective-permute-done.7.refs_2_
  41.7 4.1 %collective-permute-done.8.refs_3_ = f32[1,64,384]{2,1,0:T(8,128)S(1)} collective-permute-done((f32[1,64,384]{2,1,0:T(8,128)S(1)}, f32[1,64,384]{2,1,0:T(8,128)S(1)}, u32[]{:S(2)}, u32[]{:S(2)}) %collective-permute-start.8) | collective-permute-done | bytes 98336 | tf_op jit(solution)/shard_map/ppermute | solution.py:198
  45.8 0.0 collective-permute-done.5.refs_1_
  45.8 0.0 copy-done.1
  45.8 0.3 shard_map.66
  46.2 18.7 %all_to_all.5.all_ref = f32[16,8,128]{2,1,0:T(8,128)S(1)} all-to-all(f32[16,8,128]{2,1,0:T(8,128)S(1)} %get-tuple-element.38), channel_id=1, replica_groups=mesh['x'=4,'yh'=4,'z'=8,'yl'=2,'c'=2] {'x','yh'}, dimensions={0} | all-to-all | bytes 131072 | tf_op jit(solution)/shard_map/all_to_all | solution.py:226
  64.9 0.9 %shard_map.67 = (f32[64,384]{1,0:T(8,128)}, f32[64,384]{1,0:T(8,128)}) custom-call(f32[64,384]{1,0:T(8,128)S(1)} %get-tuple-element.36.updated_ref, f32[8,128]{1,0:T(8,128)S(1)} %get-tuple-element.37.own_ref, f32[16,8,128]{2,1,0:T(8,128)S(1)} %all_to_all.5.all_ref, f32[3,64,64]{2,1,0:T(8,128)S(1)} %get-tuple-element.39.u_ref, ...), custom_call_target="tpu_custom_call" | custom-call | tf_op jit(solution)/shard_map/pallas_call | solution.py:178
  (4 shorter events, 0.1 us)
Async XLA Ops:
  0.6 1.4 %copy-start = (bf16[1,1,1,64,12288]{4,3,2,1,0:T(8,128)(2,1)S(1)}, bf16[1,1,1,64,12288]{4,3,2,1,0:T(8,128)(2,1)}, u32[]{:S(2)}) copy-start(bf16[1,1,1,64,12288]{4,3,2,1,0:T(8,128)(2,1)} %param.4) | copy-start | bytes 4718596
  2.1 5.3 %collective-permute-start = (f32[16,64,384]{2,1,0:T(8,128)S(1)}, f32[16,64,384]{2,1,0:T(8,128)S(1)}, u32[]{:S(2)}, u32[]{:S(2)}) collective-permute-start(f32[16,64,384]{2,1,0:T(8,128)S(1)} %shard_map.60), channel_id=1, source_target_pairs={{0,1},{1,0},{2,3},{3,2},{4,5},{5,4},{6,7},{7,6},{8,9},{9,8},{10,11... | collective-permute-start | bytes 4718600 | tf_op jit(solution)/shard_map/ppermute | solution.py:198
  7.6 33.5 %copy-start.3 = (s32[1,1,6,32]{3,1,2,0:T(1,128)S(1)}, s32[1,1,6,32]{3,1,2,0:T(1,128)}, u32[]{:S(2)}) copy-start(s32[1,1,6,32]{3,1,2,0:T(1,128)} %param.6) | copy-start | bytes 2308
  7.6 33.6 %copy-start.2 = (f32[64,64]{1,0:T(8,128)S(1)}, f32[64,64]{1,0:T(8,128)}, u32[]{:S(2)}) copy-start(f32[64,64]{1,0:T(8,128)} %constant.2.clone.dct_ref) | copy-start | bytes 49156
  7.6 38.2 %copy-start.1 = (f32[1,1,64,384]{3,2,1,0:T(8,128)S(1)}, f32[1,1,64,384]{3,2,1,0:T(8,128)}, u32[]{:S(2)}) copy-start(f32[1,1,64,384]{3,2,1,0:T(8,128)} %param.5) | copy-start | bytes 294916
  7.6 18.3 %collective-permute-start.3 = (f32[4,64,384]{2,1,0:T(8,128)S(1)}, f32[4,64,384]{2,1,0:T(8,128)S(1)}, u32[]{:S(2)}, u32[]{:S(2)}) collective-permute-start(f32[4,64,384]{2,1,0:T(8,128)S(1)} %get-tuple-element.27), channel_id=1, source_target_pairs={{0,4},{1,29},{2,6},{3,31},{4,8},{5,1},{6,10},{7,3},{8,12},{9,5},{1... | collective-permute-start | bytes 1179656 | tf_op jit(solution)/shard_map/ppermute | solution.py:198
  12.1 18.2 %collective-permute-start.6 = (f32[2,64,384]{2,1,0:T(8,128)S(1)}, f32[2,64,384]{2,1,0:T(8,128)S(1)}, u32[]{:S(2)}, u32[]{:S(2)}) collective-permute-start(f32[2,64,384]{2,1,0:T(8,128)S(1)} %get-tuple-element.30), channel_id=1, source_target_pairs={{0,8},{1,25},{2,10},{3,27},{4,12},{5,29},{6,14},{7,31},{8,16},{9,1... | collective-permute-start | bytes 589832 | tf_op jit(solution)/shard_map/ppermute | solution.py:198
  18.2 19.5 %collective-permute-start.1 = (f32[2,64,384]{2,1,0:T(8,128)S(1)}, f32[2,64,384]{2,1,0:T(8,128)S(1)}, u32[]{:S(2)}, u32[]{:S(2)}) collective-permute-start(f32[2,64,384]{2,1,0:T(8,128)S(1)} %get-tuple-element.24), channel_id=1, source_target_pairs={{0,4},{1,29},{2,6},{3,31},{4,8},{5,1},{6,10},{7,3},{8,12},{9,5},{1... | collective-permute-start | bytes 589832 | tf_op jit(solution)/shard_map/ppermute | solution.py:198
  23.7 14.0 %collective-permute-start.2 = (f32[2,64,384]{2,1,0:T(8,128)S(1)}, f32[2,64,384]{2,1,0:T(8,128)S(1)}, u32[]{:S(2)}, u32[]{:S(2)}) collective-permute-start(f32[2,64,384]{2,1,0:T(8,128)S(1)} %get-tuple-element.25), channel_id=1, source_target_pairs={{0,5},{1,28},{2,7},{3,30},{4,9},{5,0},{6,11},{7,2},{8,13},{9,4},{1... | collective-permute-start | bytes 589832 | tf_op jit(solution)/shard_map/ppermute | solution.py:198
  26.0 11.7 %collective-permute-start.4 = (f32[2,64,384]{2,1,0:T(8,128)S(1)}, f32[2,64,384]{2,1,0:T(8,128)S(1)}, u32[]{:S(2)}, u32[]{:S(2)}) collective-permute-start(f32[2,64,384]{2,1,0:T(8,128)S(1)} %shard_map.62), channel_id=1, source_target_pairs={{0,9},{1,24},{2,11},{3,26},{4,13},{5,28},{6,15},{7,30},{8,17},{9,0... | collective-permute-start | bytes 589832 | tf_op jit(solution)/shard_map/ppermute | solution.py:198
  30.3 11.4 %collective-permute-start.7 = (f32[1,64,384]{2,1,0:T(8,128)S(1)}, f32[1,64,384]{2,1,0:T(8,128)S(1)}, u32[]{:S(2)}, u32[]{:S(2)}) collective-permute-start(f32[1,64,384]{2,1,0:T(8,128)S(1)} %get-tuple-element.31), channel_id=1, source_target_pairs={{0,8},{1,25},{2,10},{3,27},{4,12},{5,29},{6,14},{7,31},{8,16},{9,1... | collective-permute-start | bytes 294920 | tf_op jit(solution)/shard_map/ppermute | solution.py:198
  35.8 10.1 %collective-permute-start.8 = (f32[1,64,384]{2,1,0:T(8,128)S(1)}, f32[1,64,384]{2,1,0:T(8,128)S(1)}, u32[]{:S(2)}, u32[]{:S(2)}) collective-permute-start(f32[1,64,384]{2,1,0:T(8,128)S(1)} %get-tuple-element.32), channel_id=1, source_target_pairs={{0,10},{1,27},{2,8},{3,25},{4,14},{5,31},{6,12},{7,29},{8,18},{9,3... | collective-permute-start | bytes 294920 | tf_op jit(solution)/shard_map/ppermute | solution.py:198
  37.8 8.1 %collective-permute-start.5 = (f32[1,64,384]{2,1,0:T(8,128)S(1)}, f32[1,64,384]{2,1,0:T(8,128)S(1)}, u32[]{:S(2)}, u32[]{:S(2)}) collective-permute-start(f32[1,64,384]{2,1,0:T(8,128)S(1)} %get-tuple-element.29), channel_id=1, source_target_pairs={{0,2},{1,3},{2,0},{3,1},{4,6},{5,7},{6,4},{7,5},{8,10},{9,11},{10,... | collective-permute-start | bytes 294920 | tf_op jit(solution)/shard_map/ppermute | solution.py:198

commit v4 on v3

--- a/solution.py
+++ b/solution.py
@@ -24,6 +24,7 @@
     + [(k, part, side) for k in (1, 2) for part in range(2) for side in range(2)]
     + [(0, 0, side) for side in range(2)]
 )
+FIRST = 10
 HIGHEST = lax.Precision.HIGHEST
 
 
@@ -63,24 +64,26 @@
     return pltpu.CompilerParams(vmem_limit_bytes=32 * 1024 * 1024)
 
 
-def pick_kernel(other, grads_ref, out_ref):
+def pick_kernel(other, grads_ref, *outs):
     z = lax.axis_index("z")
     yl = lax.axis_index("yl")
     core = lax.axis_index("c")
     core = 1 - core if other else core
-    for slot, (distance, part, side) in enumerate(PLACES):
+    rows = [(out, row) for out in outs for row in range(out.shape[0])]
+    for (out, row), (distance, part, side) in zip(rows, PLACES):
         target = lax.rem(z + 8 + (1 - 2 * core) * distance, 8)
         block = 4 * target + 2 * (1 - yl if side else yl) + (1 - core if part else core)
         start = pl.multiple_of(block * WIDE, 128)
-        out_ref[slot] = grads_ref[:, pl.ds(start, WIDE)].astype(jnp.float32)
+        out[row] = grads_ref[:, pl.ds(start, WIDE)].astype(jnp.float32)
 
 
 def pick(grads, other):
+    sizes = (FIRST, len(PLACES) - FIRST)
     return pl.pallas_call(
         functools.partial(pick_kernel, other),
-        out_shape=f32(len(PLACES), BLOCK, WIDE),
+        out_shape=tuple(f32(n, BLOCK, WIDE) for n in sizes),
         in_specs=[vmem()],
-        out_specs=vmem(),
+        out_specs=(vmem(),) * len(sizes),
         compiler_params=params(),
     )(grads)
 
@@ -202,13 +205,14 @@
     grads = partial_grads.reshape(BLOCK, -1)
     momentum = momentum.reshape(BLOCK, WIDE)
 
-    got = send(pick(grads, True), c=1)
-    own = pick(grads, False)
+    first, rest = pick(grads, True)
+    first = send(first, c=1)
+    rest = send(rest, c=1)
+    own, own_rest = pick(grads, False)
     u, u_high, u_low, v_t, v_high, v_low = tables(keep_index.reshape(1, -1))
     join = lambda *slots: [[(0, i), (1, i)] for i in slots]
-    three, four, near, near_x, two, here = sums(
-        [join(0, 1, 2, 3), join(4, 5), join(6, 7), join(8, 9), join(10, 11, 12, 13), join(14, 15)], own, got
-    )
+    three, four, near, near_x = sums([join(0, 1, 2, 3), join(4, 5), join(6, 7), join(8, 9)], own, first)
+    two, here = sums([join(0, 1, 2, 3), join(4, 5)], own_rest, rest)
     three = send(three, hops=1)
     four = send(four, hops=2)
     near = send(near, hops=1)

time: 66.2 us -> 65.9 us (level)
  waiting for transfers between devices: 7.4 us -> 4.51 us
  starting transfers between devices: 35.1 us -> 37.6 us
    ppermute x9 -> x10, waiting for transfers between devices: 7.4 us -> 4.51 us  [send(): return lax.ppermute(array, FSDP, permutation(hops, yl, c))]
    ppermute x9 -> x10, starting transfers between devices: 35.1 us -> 37.6 us  [send(): return lax.ppermute(array, FSDP, permutation(hops, yl, c))]
  transfers between devices with their start and end apart: 9 -> 10, of which waited for: 3 -> 1; matrix products, arithmetic and copies ran while one was open for 0% -> 0% of each run, Pallas kernels for 1% -> 1%
where the time goes in v4:
time: 65.9 us; the launch traced here: 65.4 us
  starting transfers between devices  37.6 us (57%)
  blocking collectives  18.8 us (29%)
  waiting for transfers between devices  4.51 us (7%)
  Pallas kernels  2.16 us (3%)
  local copies, waits for them, and re-layouts  1.5 us (2%)
  between operations  0.87 us (1%)
    ppermute x10, starting transfers between devices, send(): return lax.ppermute(array, FSDP, permutation(hops, yl, c))  37.6 us
    all_to_all x1, blocking collectives, per_device(): from_all = lax.all_to_all(to_all, REP, 0, 0, tiled=True)  18.8 us
    ppermute x10, waiting for transfers between devices, send(): return lax.ppermute(array, FSDP, permutation(hops, yl, c))  4.51 us
    unnamed x8, local copies, waits for them, and re-layouts  1.42 us
  transfers between devices with their start and end apart: 10, of which 1 were waited for; matrix products, arithmetic and copies ran while one was open for 0% of the time, Pallas kernels for 1%

profile of v4, /device:TPU:8, one launch (start us, length us, event | category | flops | bytes accessed | tf_op | source)
XLA Modules:
  0.0 65.4 jit_solution(10446305227038693855)
XLA Ops:
  0.6 0.0 copy-start
  0.6 1.4 %copy-done = bf16[1,1,1,64,12288]{4,3,2,1,0:T(8,128)(2,1)S(1)} copy-done((bf16[1,1,1,64,12288]{4,3,2,1,0:T(8,128)(2,1)S(1)}, bf16[1,1,1,64,12288]{4,3,2,1,0:T(8,128)(2,1)}, u32[]{:S(2)}) %copy-start) | copy-done | bytes 1572888
  2.0 0.1 shard_map.60
  2.1 1.9 %collective-permute-start.1 = (f32[10,64,384]{2,1,0:T(8,128)S(1)}, f32[10,64,384]{2,1,0:T(8,128)S(1)}, u32[]{:S(2)}, u32[]{:S(2)}) collective-permute-start(f32[10,64,384]{2,1,0:T(8,128)S(1)} %get-tuple-element.31), channel_id=1, source_target_pairs={{0,1},{1,0},{2,3},{3,2},{4,5},{5,4},{6,7},{7,6},{8,9},{9,8},{10,11... | collective-permute-start | bytes 2949128 | tf_op jit(solution)/shard_map/ppermute | solution.py:201
  4.1 2.4 %collective-permute-start = (f32[6,64,384]{2,1,0:T(8,128)S(1)}, f32[6,64,384]{2,1,0:T(8,128)S(1)}, u32[]{:S(2)}, u32[]{:S(2)}) collective-permute-start(f32[6,64,384]{2,1,0:T(8,128)S(1)} %get-tuple-element.28), channel_id=1, source_target_pairs={{0,1},{1,0},{2,3},{3,2},{4,5},{5,4},{6,7},{7,6},{8,9},{9,8},{10,11... | collective-permute-start | bytes 1769480 | tf_op jit(solution)/shard_map/ppermute | solution.py:201
  6.5 0.1 shard_map.59
  6.6 0.0 collective-permute-done.1.refs_1_
  6.6 0.1 shard_map.62
  6.7 4.3 %collective-permute-start.4 = (f32[4,64,384]{2,1,0:T(8,128)S(1)}, f32[4,64,384]{2,1,0:T(8,128)S(1)}, u32[]{:S(2)}, u32[]{:S(2)}) collective-permute-start(f32[4,64,384]{2,1,0:T(8,128)S(1)} %get-tuple-element.35), channel_id=1, source_target_pairs={{0,4},{1,29},{2,6},{3,31},{4,8},{5,1},{6,10},{7,3},{8,12},{9,5},{1... | collective-permute-start | bytes 1179656 | tf_op jit(solution)/shard_map/ppermute | solution.py:201
  11.0 0.0 collective-permute-done.refs_1_
  11.0 0.1 shard_map.61
  11.1 0.0 copy-start.3
  11.1 0.0 copy-start.2
  11.1 0.0 copy-start.1
  11.1 6.2 %collective-permute-start.7 = (f32[2,64,384]{2,1,0:T(8,128)S(1)}, f32[2,64,384]{2,1,0:T(8,128)S(1)}, u32[]{:S(2)}, u32[]{:S(2)}) collective-permute-start(f32[2,64,384]{2,1,0:T(8,128)S(1)} %get-tuple-element.38), channel_id=1, source_target_pairs={{0,8},{1,25},{2,10},{3,27},{4,12},{5,29},{6,14},{7,31},{8,16},{9,1... | collective-permute-start | bytes 589832 | tf_op jit(solution)/shard_map/ppermute | solution.py:201
  17.4 5.5 %collective-permute-start.2 = (f32[2,64,384]{2,1,0:T(8,128)S(1)}, f32[2,64,384]{2,1,0:T(8,128)S(1)}, u32[]{:S(2)}, u32[]{:S(2)}) collective-permute-start(f32[2,64,384]{2,1,0:T(8,128)S(1)} %get-tuple-element.32), channel_id=1, source_target_pairs={{0,4},{1,29},{2,6},{3,31},{4,8},{5,1},{6,10},{7,3},{8,12},{9,5},{1... | collective-permute-start | bytes 589832 | tf_op jit(solution)/shard_map/ppermute | solution.py:201
  22.9 2.3 %collective-permute-start.3 = (f32[2,64,384]{2,1,0:T(8,128)S(1)}, f32[2,64,384]{2,1,0:T(8,128)S(1)}, u32[]{:S(2)}, u32[]{:S(2)}) collective-permute-start(f32[2,64,384]{2,1,0:T(8,128)S(1)} %get-tuple-element.33), channel_id=1, source_target_pairs={{0,5},{1,28},{2,7},{3,30},{4,9},{5,0},{6,11},{7,2},{8,13},{9,4},{1... | collective-permute-start | bytes 589832 | tf_op jit(solution)/shard_map/ppermute | solution.py:201
  25.1 0.0 collective-permute-done.4.refs_1_
  25.2 4.2 %collective-permute-start.5 = (f32[2,64,384]{2,1,0:T(8,128)S(1)}, f32[2,64,384]{2,1,0:T(8,128)S(1)}, u32[]{:S(2)}, u32[]{:S(2)}) collective-permute-start(f32[2,64,384]{2,1,0:T(8,128)S(1)} %shard_map.63), channel_id=1, source_target_pairs={{0,9},{1,24},{2,11},{3,26},{4,13},{5,28},{6,15},{7,30},{8,17},{9,0... | collective-permute-start | bytes 589832 | tf_op jit(solution)/shard_map/ppermute | solution.py:201
  29.4 0.0 collective-permute-done.7.refs_2_
  29.5 5.5 %collective-permute-start.8 = (f32[1,64,384]{2,1,0:T(8,128)S(1)}, f32[1,64,384]{2,1,0:T(8,128)S(1)}, u32[]{:S(2)}, u32[]{:S(2)}) collective-permute-start(f32[1,64,384]{2,1,0:T(8,128)S(1)} %get-tuple-element.39), channel_id=1, source_target_pairs={{0,8},{1,25},{2,10},{3,27},{4,12},{5,29},{6,14},{7,31},{8,16},{9,1... | collective-permute-start | bytes 294920 | tf_op jit(solution)/shard_map/ppermute | solution.py:201
  35.0 1.9 %collective-permute-start.9 = (f32[1,64,384]{2,1,0:T(8,128)S(1)}, f32[1,64,384]{2,1,0:T(8,128)S(1)}, u32[]{:S(2)}, u32[]{:S(2)}) collective-permute-start(f32[1,64,384]{2,1,0:T(8,128)S(1)} %get-tuple-element.40), channel_id=1, source_target_pairs={{0,10},{1,27},{2,8},{3,25},{4,14},{5,31},{6,12},{7,29},{8,18},{9,3... | collective-permute-start | bytes 294920 | tf_op jit(solution)/shard_map/ppermute | solution.py:201
  36.9 0.0 collective-permute-done.2.refs_1_
  36.9 0.0 collective-permute-done.3.refs_2_
  36.9 0.0 collective-permute-done.5.refs_3_
  37.0 3.4 %collective-permute-start.6 = (f32[1,64,384]{2,1,0:T(8,128)S(1)}, f32[1,64,384]{2,1,0:T(8,128)S(1)}, u32[]{:S(2)}, u32[]{:S(2)}) collective-permute-start(f32[1,64,384]{2,1,0:T(8,128)S(1)} %get-tuple-element.37), channel_id=1, source_target_pairs={{0,2},{1,3},{2,0},{3,1},{4,6},{5,7},{6,4},{7,5},{8,10},{9,11},{10,... | collective-permute-start | bytes 294920 | tf_op jit(solution)/shard_map/ppermute | solution.py:201
  40.4 0.0 copy-done.3
  40.4 0.1 reshape.21.index_ref
  40.5 0.0 copy-done.2
  40.5 0.5 shard_map.66
  40.9 0.0 collective-permute-done.8.refs_2_
  40.9 4.5 %collective-permute-done.9.refs_3_ = f32[1,64,384]{2,1,0:T(8,128)S(1)} collective-permute-done((f32[1,64,384]{2,1,0:T(8,128)S(1)}, f32[1,64,384]{2,1,0:T(8,128)S(1)}, u32[]{:S(2)}, u32[]{:S(2)}) %collective-permute-start.9) | collective-permute-done | bytes 98336 | tf_op jit(solution)/shard_map/ppermute | solution.py:201
  45.4 0.0 collective-permute-done.6.refs_1_
  45.4 0.0 copy-done.1
  45.4 0.3 shard_map.67
  45.8 18.8 %all_to_all.5.all_ref = f32[16,8,128]{2,1,0:T(8,128)S(1)} all-to-all(f32[16,8,128]{2,1,0:T(8,128)S(1)} %get-tuple-element.46), channel_id=1, replica_groups=mesh['x'=4,'yh'=4,'z'=8,'yl'=2,'c'=2] {'x','yh'}, dimensions={0} | all-to-all | bytes 131072 | tf_op jit(solution)/shard_map/all_to_all | solution.py:230
  64.6 0.9 %shard_map.68 = (f32[64,384]{1,0:T(8,128)}, f32[64,384]{1,0:T(8,128)}) custom-call(f32[64,384]{1,0:T(8,128)S(1)} %get-tuple-element.44.updated_ref, f32[8,128]{1,0:T(8,128)S(1)} %get-tuple-element.45.own_ref, f32[16,8,128]{2,1,0:T(8,128)S(1)} %all_to_all.5.all_ref, f32[3,64,64]{2,1,0:T(8,128)S(1)} %get-tuple-element.47.u_ref, ...), custom_call_target="tpu_custom_call" | custom-call | tf_op jit(solution)/shard_map/pallas_call | solution.py:181
  (4 shorter events, 0.1 us)
Async XLA Ops:
  0.6 1.4 %copy-start = (bf16[1,1,1,64,12288]{4,3,2,1,0:T(8,128)(2,1)S(1)}, bf16[1,1,1,64,12288]{4,3,2,1,0:T(8,128)(2,1)}, u32[]{:S(2)}) copy-start(bf16[1,1,1,64,12288]{4,3,2,1,0:T(8,128)(2,1)} %param.4) | copy-start | bytes 4718596
  2.1 4.5 %collective-permute-start.1 = (f32[10,64,384]{2,1,0:T(8,128)S(1)}, f32[10,64,384]{2,1,0:T(8,128)S(1)}, u32[]{:S(2)}, u32[]{:S(2)}) collective-permute-start(f32[10,64,384]{2,1,0:T(8,128)S(1)} %get-tuple-element.31), channel_id=1, source_target_pairs={{0,1},{1,0},{2,3},{3,2},{4,5},{5,4},{6,7},{7,6},{8,9},{9,8},{10,11... | collective-permute-start | bytes 2949128 | tf_op jit(solution)/shard_map/ppermute | solution.py:201
  4.1 7.0 %collective-permute-start = (f32[6,64,384]{2,1,0:T(8,128)S(1)}, f32[6,64,384]{2,1,0:T(8,128)S(1)}, u32[]{:S(2)}, u32[]{:S(2)}) collective-permute-start(f32[6,64,384]{2,1,0:T(8,128)S(1)} %get-tuple-element.28), channel_id=1, source_target_pairs={{0,1},{1,0},{2,3},{3,2},{4,5},{5,4},{6,7},{7,6},{8,9},{9,8},{10,11... | collective-permute-start | bytes 1769480 | tf_op jit(solution)/shard_map/ppermute | solution.py:201
  6.7 18.4 %collective-permute-start.4 = (f32[4,64,384]{2,1,0:T(8,128)S(1)}, f32[4,64,384]{2,1,0:T(8,128)S(1)}, u32[]{:S(2)}, u32[]{:S(2)}) collective-permute-start(f32[4,64,384]{2,1,0:T(8,128)S(1)} %get-tuple-element.35), channel_id=1, source_target_pairs={{0,4},{1,29},{2,6},{3,31},{4,8},{5,1},{6,10},{7,3},{8,12},{9,5},{1... | collective-permute-start | bytes 1179656 | tf_op jit(solution)/shard_map/ppermute | solution.py:201
  11.1 29.2 %copy-start.3 = (s32[1,1,6,32]{3,1,2,0:T(1,128)S(1)}, s32[1,1,6,32]{3,1,2,0:T(1,128)}, u32[]{:S(2)}) copy-start(s32[1,1,6,32]{3,1,2,0:T(1,128)} %param.6) | copy-start | bytes 2308
  11.1 29.3 %copy-start.2 = (f32[64,64]{1,0:T(8,128)S(1)}, f32[64,64]{1,0:T(8,128)}, u32[]{:S(2)}) copy-start(f32[64,64]{1,0:T(8,128)} %constant.2.clone.dct_ref) | copy-start | bytes 49156
  11.1 34.3 %copy-start.1 = (f32[1,1,64,384]{3,2,1,0:T(8,128)S(1)}, f32[1,1,64,384]{3,2,1,0:T(8,128)}, u32[]{:S(2)}) copy-start(f32[1,1,64,384]{3,2,1,0:T(8,128)} %param.5) | copy-start | bytes 294916
  11.1 18.3 %collective-permute-start.7 = (f32[2,64,384]{2,1,0:T(8,128)S(1)}, f32[2,64,384]{2,1,0:T(8,128)S(1)}, u32[]{:S(2)}, u32[]{:S(2)}) collective-permute-start(f32[2,64,384]{2,1,0:T(8,128)S(1)} %get-tuple-element.38), channel_id=1, source_target_pairs={{0,8},{1,25},{2,10},{3,27},{4,12},{5,29},{6,14},{7,31},{8,16},{9,1... | collective-permute-start | bytes 589832 | tf_op jit(solution)/shard_map/ppermute | solution.py:201
  17.4 19.5 %collective-permute-start.2 = (f32[2,64,384]{2,1,0:T(8,128)S(1)}, f32[2,64,384]{2,1,0:T(8,128)S(1)}, u32[]{:S(2)}, u32[]{:S(2)}) collective-permute-start(f32[2,64,384]{2,1,0:T(8,128)S(1)} %get-tuple-element.32), channel_id=1, source_target_pairs={{0,4},{1,29},{2,6},{3,31},{4,8},{5,1},{6,10},{7,3},{8,12},{9,5},{1... | collective-permute-start | bytes 589832 | tf_op jit(solution)/shard_map/ppermute | solution.py:201
  22.9 14.0 %collective-permute-start.3 = (f32[2,64,384]{2,1,0:T(8,128)S(1)}, f32[2,64,384]{2,1,0:T(8,128)S(1)}, u32[]{:S(2)}, u32[]{:S(2)}) collective-permute-start(f32[2,64,384]{2,1,0:T(8,128)S(1)} %get-tuple-element.33), channel_id=1, source_target_pairs={{0,5},{1,28},{2,7},{3,30},{4,9},{5,0},{6,11},{7,2},{8,13},{9,4},{1... | collective-permute-start | bytes 589832 | tf_op jit(solution)/shard_map/ppermute | solution.py:201
  25.2 11.7 %collective-permute-start.5 = (f32[2,64,384]{2,1,0:T(8,128)S(1)}, f32[2,64,384]{2,1,0:T(8,128)S(1)}, u32[]{:S(2)}, u32[]{:S(2)}) collective-permute-start(f32[2,64,384]{2,1,0:T(8,128)S(1)} %shard_map.63), channel_id=1, source_target_pairs={{0,9},{1,24},{2,11},{3,26},{4,13},{5,28},{6,15},{7,30},{8,17},{9,0... | collective-permute-start | bytes 589832 | tf_op jit(solution)/shard_map/ppermute | solution.py:201
  29.5 11.5 %collective-permute-start.8 = (f32[1,64,384]{2,1,0:T(8,128)S(1)}, f32[1,64,384]{2,1,0:T(8,128)S(1)}, u32[]{:S(2)}, u32[]{:S(2)}) collective-permute-start(f32[1,64,384]{2,1,0:T(8,128)S(1)} %get-tuple-element.39), channel_id=1, source_target_pairs={{0,8},{1,25},{2,10},{3,27},{4,12},{5,29},{6,14},{7,31},{8,16},{9,1... | collective-permute-start | bytes 294920 | tf_op jit(solution)/shard_map/ppermute | solution.py:201
  35.0 10.5 %collective-permute-start.9 = (f32[1,64,384]{2,1,0:T(8,128)S(1)}, f32[1,64,384]{2,1,0:T(8,128)S(1)}, u32[]{:S(2)}, u32[]{:S(2)}) collective-permute-start(f32[1,64,384]{2,1,0:T(8,128)S(1)} %get-tuple-element.40), channel_id=1, source_target_pairs={{0,10},{1,27},{2,8},{3,25},{4,14},{5,31},{6,12},{7,29},{8,18},{9,3... | collective-permute-start | bytes 294920 | tf_op jit(solution)/shard_map/ppermute | solution.py:201
  37.0 8.5 %collective-permute-start.6 = (f32[1,64,384]{2,1,0:T(8,128)S(1)}, f32[1,64,384]{2,1,0:T(8,128)S(1)}, u32[]{:S(2)}, u32[]{:S(2)}) collective-permute-start(f32[1,64,384]{2,1,0:T(8,128)S(1)} %get-tuple-element.37), channel_id=1, source_target_pairs={{0,2},{1,3},{2,0},{3,1},{4,6},{5,7},{6,4},{7,5},{8,10},{9,11},{10,... | collective-permute-start | bytes 294920 | tf_op jit(solution)/shard_map/ppermute | solution.py:201
